TPU v7x, 32 devices: a whole 2x2x4 slice. The times are simulated.
32 devices in a mesh: section: 4 (over z), ctx: 8 (over y, x, core).
Axes of the slice: x: 2, y: 2, z: 4, core: 2. Of those that a mesh axis runs over, the one named last changes fastest.
Arguments:
- spins: int32 [4, 1024], replicated, may hold values from 0 to 1
- block_mask: int32 [8, 8], P('ctx'), may hold values from 0 to 1, as said below
- tok_embed: float32 [3, 1024], replicated, may hold values from -6 to 6
- pos_embed: bfloat16 [1024, 1024], P('ctx'), may hold values from -6 to 6
- norm1_gain: float32 [4, 1024], P('section'), may hold values from 0.1 to 1.9
- w_qkv: bfloat16 [4, 1024, 3072], P('section')
- w_out: bfloat16 [4, 1024, 1024], P('section'), may hold values from -0.1875 to 0.1875
- norm2_gain: float32 [4, 1024], P('section'), may hold values from 0.1 to 1.9
- w_up: bfloat16 [4, 1024, 2048], P('section'), may hold values from -0.1875 to 0.1875
- w_down: bfloat16 [4, 2048, 1024], P('section'), may hold values from -0.125 to 0.125
- w_head: float32 [1024], replicated, may hold values from -0.1875 to 0.1875
Outputs:
- log_amplitude: float32 [4, 1024], P('section', 'ctx')
Inputs may be any that keep to these rules, and one draw needn't show every extreme that they name: block_mask[q, k] is 1 where k = q, and where k = q - 1; where q - k = 2 ** j with 1 <= j < 3 it is 0 or 1; it is 0 everywhere else.
All inputs are finite; a program needn't handle non-finite values.
Results may differ from a plain program's by a relative error of at most 0.012.
Values may be sent and summed in bfloat16 or wider, within the bound.
A program may use at most 64 MiB of HBM per device.

v0:
```python
import math

import jax
import jax.numpy as jnp
from jax import lax
from jax.sharding import PartitionSpec as P

HEADS = 16
NDIL = 3


def from_behind(value, axis, by):
    devices = lax.axis_size(axis)
    pairs = [(i, i + by) for i in range(devices) if 0 <= i + by < devices]
    return lax.ppermute(value, axis, pairs)


def rms_normed(vector):
    return vector * lax.rsqrt(jnp.mean(vector * vector, axis=-1, keepdims=True) + 1e-05)


def body(
    spins,
    block_mask,
    tok_embed,
    pos_embed,
    norm1_gain,
    w_qkv,
    w_out,
    norm2_gain,
    w_up,
    w_down,
    w_head,
):
    segment_list = lax.axis_size("section")
    segment_index = lax.axis_index("section")
    ctx_index = lax.axis_index("ctx")
    block_len, model_width = pos_embed.shape
    seq_count = spins.shape[0] // segment_list
    head_count = HEADS
    head_dim = model_width // head_count
    row_count = seq_count * block_len
    block_count = block_mask.shape[1]
    site_start = ctx_index * block_len
    shifted = jnp.concatenate([jnp.full((spins.shape[0], 1), 2, jnp.int32), spins[:, :-1]], axis=1)
    prev_spins = lax.dynamic_slice_in_dim(shifted, site_start, block_len, 1)
    own_spins = lax.dynamic_slice_in_dim(spins, site_start, block_len, 1)
    gain_one = norm1_gain[0]
    gain_two = norm2_gain[0]
    weight_qkv = w_qkv[0]
    weight_out = w_out[0]
    weight_up = w_up[0]
    weight_down = w_down[0]
    distances = [1 << level_index for level_index in range(NDIL)]
    mask_row = block_mask[0]
    columns = jnp.arange(block_count, dtype=jnp.int32)
    positions = jnp.arange(block_len, dtype=jnp.int32)
    causal = positions[None, :] <= positions[:, None]
    flags = []
    for distance in distances:
        listed = jnp.sum(jnp.where(columns == ctx_index - distance, mask_row, 0)) > 0
        flags.append(jnp.broadcast_to((ctx_index - distance >= 0) & listed, (block_len, block_len)))
    key_mask = jnp.concatenate([causal] + flags, axis=1)
    blank_rows = jnp.zeros((row_count, model_width), jnp.bfloat16)

    def embed(micro_index):
        tokens = lax.dynamic_slice_in_dim(prev_spins, micro_index * seq_count, seq_count, 0)[
            ..., None
        ]
        token_rows = jnp.where(
            tokens == 0, tok_embed[0], jnp.where(tokens == 1, tok_embed[1], tok_embed[2])
        )
        summed = token_rows + pos_embed.astype(jnp.float32)[None]
        return summed.astype(jnp.bfloat16).reshape(row_count, model_width)

    def project(normed_rows):
        projected = jnp.dot(normed_rows, weight_qkv, preferred_element_type=jnp.float32)
        return (
            projected[:, :model_width].astype(jnp.bfloat16),
            projected[:, model_width : 2 * model_width].astype(jnp.bfloat16),
            projected[:, 2 * model_width :].astype(jnp.bfloat16),
        )

    def to_heads(matrix):
        return matrix.reshape(seq_count, block_len, head_count, head_dim)

    def finish(layer_in, queries, key_list, value_list):
        key_all = jnp.concatenate([to_heads(member) for member in key_list], axis=1)
        value_all = jnp.concatenate([to_heads(member) for member in value_list], axis=1)
        scores = jnp.einsum(
            "sqhd,skhd->shqk", to_heads(queries), key_all, preferred_element_type=jnp.float32
        ) / math.sqrt(head_dim)
        scores = jnp.where(key_mask[None, None], scores, -jnp.inf)
        weights = jax.nn.softmax(scores, axis=-1).astype(jnp.bfloat16)
        attended = jnp.einsum(
            "shqk,skhd->sqhd", weights, value_all, preferred_element_type=jnp.float32
        )
        attended = attended.astype(jnp.bfloat16).reshape(row_count, model_width)
        hidden = layer_in.astype(jnp.float32) + jnp.dot(
            attended, weight_out, preferred_element_type=jnp.float32
        )
        lifted = (rms_normed(hidden) * gain_two).astype(jnp.bfloat16)
        activated = jax.nn.gelu(
            jnp.dot(lifted, weight_up, preferred_element_type=jnp.float32)
        ).astype(jnp.bfloat16)
        return (
            hidden + jnp.dot(activated, weight_down, preferred_element_type=jnp.float32)
        ).astype(jnp.bfloat16)

    def skip_project(normed_rows):
        return (blank_rows, blank_rows, blank_rows)

    def skip_finish(layer_in, queries, key_list, value_list):
        return blank_rows

    def section_step(iteration_state, tick_index):
        incoming_part, carried_value = iteration_state
        micro_now = tick_index - segment_index
        active = (micro_now >= 0) & (micro_now < segment_list)
        embedded = embed(jnp.clip(tick_index, 0, segment_list - 1))
        layer_in = jnp.where(segment_index == 0, embedded, incoming_part)
        normed_rows = (rms_normed(layer_in.astype(jnp.float32)) * gain_one).astype(jnp.bfloat16)
        queries, key_own, value_own = lax.cond(active, project, skip_project, normed_rows)
        key_list = [key_own]
        value_list = [value_own]
        for distance in distances:
            key_far, value_far = from_behind((key_own, value_own), "ctx", distance)
            key_list.append(key_far)
            value_list.append(value_far)
        layer_out = lax.cond(active, finish, skip_finish, layer_in, queries, key_list, value_list)
        handed_over = from_behind(layer_out, "section", 1)
        final_rows = rms_normed(layer_out.astype(jnp.float32))
        logits = jnp.dot(final_rows, w_head, precision=lax.Precision.HIGHEST).reshape(
            seq_count, block_len
        )
        spins_now = lax.dynamic_slice_in_dim(
            own_spins, jnp.clip(micro_now, 0, segment_list - 1) * seq_count, seq_count, 0
        )
        per_site_terms = math.log(2.0) - jax.nn.softplus(
            (1.0 - 2.0 * spins_now.astype(jnp.float32)) * logits
        )
        returned_rows = from_behind(carried_value, "section", -1)
        carried_value = jnp.where(segment_index == segment_list - 1, per_site_terms, returned_rows)
        return ((handed_over, carried_value), None)

    tick_count = 2 * segment_list - 1
    initial = (blank_rows, jnp.zeros((seq_count, block_len), jnp.float32))
    closing_state, unused = lax.scan(section_step, initial, jnp.arange(tick_count, dtype=jnp.int32))
    carried_value = closing_state[1]
    running_total = jnp.cumsum(carried_value, axis=1)
    totals = running_total[:, -1]
    ctx_count = lax.axis_size("ctx")
    gathered = lax.all_gather(totals, "ctx", axis=0, tiled=True).reshape(ctx_count, seq_count)
    earlier = (jnp.arange(ctx_count, dtype=jnp.int32) < ctx_index)[:, None]
    offset = jnp.sum(jnp.where(earlier, gathered, 0.0), axis=0)
    return 0.5 * (running_total + offset[:, None])


def solution(mesh):
    return jax.shard_map(
        body,
        mesh=mesh,
        in_specs=(
            P(),
            P("ctx", None),
            P(),
            P("ctx", None),
            P("section", None),
            P("section", None, None),
            P("section", None, None),
            P("section", None),
            P("section", None, None),
            P("section", None, None),
            P(),
        ),
        out_specs=P("section", "ctx"),
        check_vma=False,
    )
```

profile of v0, /device:TPU:29, one launch (start us, length us, event | category | flops | bytes accessed | tf_op | source)
XLA Modules:
  0.0 532.3 jit_solution(1574304555946233455)
XLA Ops:
  4.6 510.5 %while.14 = (s32[]{:T(128)}, bf16[128,1024]{1,0:T(8,128)(2,1)S(1)}, f32[1,128]{1,0:T(1,128)S(1)}, s32[7]{0:T(128)S(1)}, s32[]{:T(128)}, /*index=5*/pred[]{:T(512...) while((s32[]{:T(128)}, bf16[128,1024]{1,0:T(8,128)(2,1)S(1)}, ...), condition=%wide.region_13.14_spmd.clone, body=%wide.region_3.13_spmd.clone.sunk | while | flops 2440563456 | bytes 63615444 | solution.py:148
  11.3 3.7 collective-permute-start
  27.8 12.1 %collective-permute-done.2 = bf16[128,1024]{0,1:T(8,128)(2,1)} collective-permute-done((bf16[128,1024]{0,1:T(8,128)(2,1)S(1)}, bf16[128,1024]{0,1:T(8,128)(2,1)}, u32[]{:S(2)}, u32[]{:S(2)}) %collective-permute-start.2) | collective-permute-done | bytes 262176 | tf_op jit(solution)/shard_map/while/body/eval_jaxpr/ppermute | solution.py:15
  39.9 5.6 %collective-permute-done.5 = bf16[128,1024]{0,1:T(8,128)(2,1)} collective-permute-done((bf16[128,1024]{0,1:T(8,128)(2,1)S(1)}, bf16[128,1024]{0,1:T(8,128)(2,1)}, u32[]{:S(2)}, u32[]{:S(2)}) %collective-permute-start.5) | collective-permute-done | bytes 262176 | tf_op jit(solution)/shard_map/while/body/eval_jaxpr/ppermute | solution.py:15
  48.2 7.6 %collective-permute-done.6 = bf16[128,1024]{1,0:T(8,128)(2,1)S(1)} collective-permute-done((bf16[128,1024]{1,0:T(8,128)(2,1)}, bf16[128,1024]{1,0:T(8,128)(2,1)S(1)}, u32[]{:S(2)}, u32[]{:S(2)}) %collective-permute-start.6) | collective-permute-done | bytes 262176 | tf_op jit(solution)/shard_map/while/body/eval_jaxpr/ppermute | solution.py:15
  72.8 4.7 collective-permute-done.1
  79.6 12.2 %collective-permute-done.2 = bf16[128,1024]{0,1:T(8,128)(2,1)} collective-permute-done((bf16[128,1024]{0,1:T(8,128)(2,1)S(1)}, bf16[128,1024]{0,1:T(8,128)(2,1)}, u32[]{:S(2)}, u32[]{:S(2)}) %collective-permute-start.2) | collective-permute-done | bytes 262176 | tf_op jit(solution)/shard_map/while/body/eval_jaxpr/ppermute | solution.py:15
  91.8 5.5 %collective-permute-done.5 = bf16[128,1024]{0,1:T(8,128)(2,1)} collective-permute-done((bf16[128,1024]{0,1:T(8,128)(2,1)S(1)}, bf16[128,1024]{0,1:T(8,128)(2,1)}, u32[]{:S(2)}, u32[]{:S(2)}) %collective-permute-start.5) | collective-permute-done | bytes 262176 | tf_op jit(solution)/shard_map/while/body/eval_jaxpr/ppermute | solution.py:15
  100.0 14.0 %collective-permute-done.6 = bf16[128,1024]{1,0:T(8,128)(2,1)S(1)} collective-permute-done((bf16[128,1024]{1,0:T(8,128)(2,1)}, bf16[128,1024]{1,0:T(8,128)(2,1)S(1)}, u32[]{:S(2)}, u32[]{:S(2)}) %collective-permute-start.6) | collective-permute-done | bytes 262176 | tf_op jit(solution)/shard_map/while/body/eval_jaxpr/ppermute | solution.py:15
  131.1 4.6 collective-permute-done.1
  135.8 41.5 %collective-permute-start.7 = (f32[1,128]{1,0:T(1,128)S(1)}, f32[1,128]{1,0:T(1,128)S(1)}, u32[]{:S(2)}, u32[]{:S(2)}) collective-permute-start(f32[1,128]{1,0:T(1,128)S(1)} %broadcast_select_fusion.4), channel_id=1, source_target_pairs={{8,0},{16,8},{24,16},{9,1},{17,9},{25,17},{10,2},{18,10},{26,18},{... | collective-permute-start | bytes 1544 | tf_op jit(solution)/shard_map/while/body/eval_jaxpr/ppermute | solution.py:15
  180.1 40.7 %collective-permute-done.6 = bf16[128,1024]{1,0:T(8,128)(2,1)S(1)} collective-permute-done((bf16[128,1024]{1,0:T(8,128)(2,1)}, bf16[128,1024]{1,0:T(8,128)(2,1)S(1)}, u32[]{:S(2)}, u32[]{:S(2)}) %collective-permute-start.6) | collective-permute-done | bytes 262176 | tf_op jit(solution)/shard_map/while/body/eval_jaxpr/ppermute | solution.py:15
  225.9 7.1 %conditional.6 = (bf16[128,1024]{1,0:T(8,128)(2,1)S(1)}, bf16[128,1024]{1,0:T(8,128)(2,1)}, bf16[128,1024]{1,0:T(8,128)(2,1)}, bf16[128,1024]{0,1:T(8,128)(2,1)S(1)}, bf16[128,1024]{0,1:T(8,128)(2,1)S(1)}) conditional(s32[]{:T(128)} %convert_element_type.118, () %tuple.77, (bf16[128,1024]{1,0:T(8,128)(2,1)S(1)}, bf16[1024,3072]{1,0:T(8,128)(2,1)}) %tuple.78), branch_computations={%region_5.5_spmd, %region_6.6_spmd} | conditional | flops 805699584 | bytes 9961512 | solution.py:123
  225.9 3.9 convolution_convert_fusion
  243.4 4.2 collective-permute-done.1
  251.0 10.9 %collective-permute-done.2 = bf16[128,1024]{0,1:T(8,128)(2,1)} collective-permute-done((bf16[128,1024]{0,1:T(8,128)(2,1)S(1)}, bf16[128,1024]{0,1:T(8,128)(2,1)}, u32[]{:S(2)}, u32[]{:S(2)}) %collective-permute-start.2) | collective-permute-done | bytes 262176 | tf_op jit(solution)/shard_map/while/body/eval_jaxpr/ppermute | solution.py:15
  261.9 5.5 %collective-permute-done.5 = bf16[128,1024]{0,1:T(8,128)(2,1)} collective-permute-done((bf16[128,1024]{0,1:T(8,128)(2,1)S(1)}, bf16[128,1024]{0,1:T(8,128)(2,1)}, u32[]{:S(2)}, u32[]{:S(2)}) %collective-permute-start.5) | collective-permute-done | bytes 262176 | tf_op jit(solution)/shard_map/while/body/eval_jaxpr/ppermute | solution.py:15
  267.4 17.1 %conditional.7 = (bf16[128,1024]{1,0:T(8,128)(2,1)}, f32[128,1024]{1,0:T(8,128)S(1)}, f32[128,1]{0,1:T(1,128)S(1)}) conditional(s32[]{:T(128)} %convert_element_type.118, () %tuple.76, (bf16[128,1024]{1,0:T(8,128)(2,1)S(1)}, bf16[128,1024]{1,0:T(8,128)(2,1)}, bf16[128,1024]{0,1:T(8,128)(2,1)}, bf16[128,1024]{0,1:T(8,128)(2,1)}, ...), branch_computations={%region_7.7_spmd, %region_8.12_spmd} | conditional | flops 1631453696 | bytes 34953780 | solution.py:130
  270.6 3.6 fusion.62
  278.7 5.8 %multiply_reduce_fusion = (f32[128]{0:T(128)S(1)}, f32[128,1024]{1,0:T(8,128)S(1)}, bf16[128,1024]{1,0:T(8,128)(2,1)}) fusion(f32[128,1024]{1,0:T(8,128)S(1)} %get-tuple-element.364, bf16[2048,1024]{1,0:T(8,128)(2,1)} %get-tuple-element.201, bf16[1024,2048]{1,0:T(8,128)(2,1)} %get-tuple-element.200, f32[1024]{0:T(1024)S(1)} %bitcast.100, ...), kind=kOutput, calls=%fused_computation.38 | convolution fusion | flops 1077149568 | bytes 9704448 | tf_op jit(solution)/shard_map/while/body/eval_jaxpr/cond/branch_1_fun/dot_general | solution.py:107
  286.5 7.7 %collective-permute-done.6 = bf16[128,1024]{1,0:T(8,128)(2,1)S(1)} collective-permute-done((bf16[128,1024]{1,0:T(8,128)(2,1)}, bf16[128,1024]{1,0:T(8,128)(2,1)S(1)}, u32[]{:S(2)}, u32[]{:S(2)}) %collective-permute-start.6) | collective-permute-done | bytes 262176 | tf_op jit(solution)/shard_map/while/body/eval_jaxpr/ppermute | solution.py:15
  299.2 7.1 %conditional.6 = (bf16[128,1024]{1,0:T(8,128)(2,1)S(1)}, bf16[128,1024]{1,0:T(8,128)(2,1)}, bf16[128,1024]{1,0:T(8,128)(2,1)}, bf16[128,1024]{0,1:T(8,128)(2,1)S(1)}, bf16[128,1024]{0,1:T(8,128)(2,1)S(1)}) conditional(s32[]{:T(128)} %convert_element_type.118, () %tuple.77, (bf16[128,1024]{1,0:T(8,128)(2,1)S(1)}, bf16[1024,3072]{1,0:T(8,128)(2,1)}) %tuple.78), branch_computations={%region_5.5_spmd, %region_6.6_spmd} | conditional | flops 805699584 | bytes 9961512 | solution.py:123
  299.2 3.9 convolution_convert_fusion
  316.7 4.6 collective-permute-done.1
  324.6 10.9 %collective-permute-done.2 = bf16[128,1024]{0,1:T(8,128)(2,1)} collective-permute-done((bf16[128,1024]{0,1:T(8,128)(2,1)S(1)}, bf16[128,1024]{0,1:T(8,128)(2,1)}, u32[]{:S(2)}, u32[]{:S(2)}) %collective-permute-start.2) | collective-permute-done | bytes 262176 | tf_op jit(solution)/shard_map/while/body/eval_jaxpr/ppermute | solution.py:15
  335.6 5.5 %collective-permute-done.5 = bf16[128,1024]{0,1:T(8,128)(2,1)} collective-permute-done((bf16[128,1024]{0,1:T(8,128)(2,1)S(1)}, bf16[128,1024]{0,1:T(8,128)(2,1)}, u32[]{:S(2)}, u32[]{:S(2)}) %collective-permute-start.5) | collective-permute-done | bytes 262176 | tf_op jit(solution)/shard_map/while/body/eval_jaxpr/ppermute | solution.py:15
  341.1 17.1 %conditional.7 = (bf16[128,1024]{1,0:T(8,128)(2,1)}, f32[128,1024]{1,0:T(8,128)S(1)}, f32[128,1]{0,1:T(1,128)S(1)}) conditional(s32[]{:T(128)} %convert_element_type.118, () %tuple.76, (bf16[128,1024]{1,0:T(8,128)(2,1)S(1)}, bf16[128,1024]{1,0:T(8,128)(2,1)}, bf16[128,1024]{0,1:T(8,128)(2,1)}, bf16[128,1024]{0,1:T(8,128)(2,1)}, ...), branch_computations={%region_7.7_spmd, %region_8.12_spmd} | conditional | flops 1631453696 | bytes 34953780 | solution.py:130
  344.2 3.6 fusion.62
  352.4 5.8 %multiply_reduce_fusion = (f32[128]{0:T(128)S(1)}, f32[128,1024]{1,0:T(8,128)S(1)}, bf16[128,1024]{1,0:T(8,128)(2,1)}) fusion(f32[128,1024]{1,0:T(8,128)S(1)} %get-tuple-element.364, bf16[2048,1024]{1,0:T(8,128)(2,1)} %get-tuple-element.201, bf16[1024,2048]{1,0:T(8,128)(2,1)} %get-tuple-element.200, f32[1024]{0:T(1024)S(1)} %bitcast.100, ...), kind=kOutput, calls=%fused_computation.38 | convolution fusion | flops 1077149568 | bytes 9704448 | tf_op jit(solution)/shard_map/while/body/eval_jaxpr/cond/branch_1_fun/dot_general | solution.py:107
  360.1 7.7 %collective-permute-done.6 = bf16[128,1024]{1,0:T(8,128)(2,1)S(1)} collective-permute-done((bf16[128,1024]{1,0:T(8,128)(2,1)}, bf16[128,1024]{1,0:T(8,128)(2,1)S(1)}, u32[]{:S(2)}, u32[]{:S(2)}) %collective-permute-start.6) | collective-permute-done | bytes 262176 | tf_op jit(solution)/shard_map/while/body/eval_jaxpr/ppermute | solution.py:15
  372.9 7.1 %conditional.6 = (bf16[128,1024]{1,0:T(8,128)(2,1)S(1)}, bf16[128,1024]{1,0:T(8,128)(2,1)}, bf16[128,1024]{1,0:T(8,128)(2,1)}, bf16[128,1024]{0,1:T(8,128)(2,1)S(1)}, bf16[128,1024]{0,1:T(8,128)(2,1)S(1)}) conditional(s32[]{:T(128)} %convert_element_type.118, () %tuple.77, (bf16[128,1024]{1,0:T(8,128)(2,1)S(1)}, bf16[1024,3072]{1,0:T(8,128)(2,1)}) %tuple.78), branch_computations={%region_5.5_spmd, %region_6.6_spmd} | conditional | flops 805699584 | bytes 9961512 | solution.py:123
  372.9 3.9 convolution_convert_fusion
  390.3 4.6 collective-permute-done.1
  398.3 10.9 %collective-permute-done.2 = bf16[128,1024]{0,1:T(8,128)(2,1)} collective-permute-done((bf16[128,1024]{0,1:T(8,128)(2,1)S(1)}, bf16[128,1024]{0,1:T(8,128)(2,1)}, u32[]{:S(2)}, u32[]{:S(2)}) %collective-permute-start.2) | collective-permute-done | bytes 262176 | tf_op jit(solution)/shard_map/while/body/eval_jaxpr/ppermute | solution.py:15
  409.2 5.5 %collective-permute-done.5 = bf16[128,1024]{0,1:T(8,128)(2,1)} collective-permute-done((bf16[128,1024]{0,1:T(8,128)(2,1)S(1)}, bf16[128,1024]{0,1:T(8,128)(2,1)}, u32[]{:S(2)}, u32[]{:S(2)}) %collective-permute-start.5) | collective-permute-done | bytes 262176 | tf_op jit(solution)/shard_map/while/body/eval_jaxpr/ppermute | solution.py:15
  414.7 17.1 %conditional.7 = (bf16[128,1024]{1,0:T(8,128)(2,1)}, f32[128,1024]{1,0:T(8,128)S(1)}, f32[128,1]{0,1:T(1,128)S(1)}) conditional(s32[]{:T(128)} %convert_element_type.118, () %tuple.76, (bf16[128,1024]{1,0:T(8,128)(2,1)S(1)}, bf16[128,1024]{1,0:T(8,128)(2,1)}, bf16[128,1024]{0,1:T(8,128)(2,1)}, bf16[128,1024]{0,1:T(8,128)(2,1)}, ...), branch_computations={%region_7.7_spmd, %region_8.12_spmd} | conditional | flops 1631453696 | bytes 34953780 | solution.py:130
  417.9 3.6 fusion.62
  426.1 5.8 %multiply_reduce_fusion = (f32[128]{0:T(128)S(1)}, f32[128,1024]{1,0:T(8,128)S(1)}, bf16[128,1024]{1,0:T(8,128)(2,1)}) fusion(f32[128,1024]{1,0:T(8,128)S(1)} %get-tuple-element.364, bf16[2048,1024]{1,0:T(8,128)(2,1)} %get-tuple-element.201, bf16[1024,2048]{1,0:T(8,128)(2,1)} %get-tuple-element.200, f32[1024]{0:T(1024)S(1)} %bitcast.100, ...), kind=kOutput, calls=%fused_computation.38 | convolution fusion | flops 1077149568 | bytes 9704448 | tf_op jit(solution)/shard_map/while/body/eval_jaxpr/cond/branch_1_fun/dot_general | solution.py:107
  433.8 7.7 %collective-permute-done.6 = bf16[128,1024]{1,0:T(8,128)(2,1)S(1)} collective-permute-done((bf16[128,1024]{1,0:T(8,128)(2,1)}, bf16[128,1024]{1,0:T(8,128)(2,1)S(1)}, u32[]{:S(2)}, u32[]{:S(2)}) %collective-permute-start.6) | collective-permute-done | bytes 262176 | tf_op jit(solution)/shard_map/while/body/eval_jaxpr/ppermute | solution.py:15
  446.5 7.1 %conditional.6 = (bf16[128,1024]{1,0:T(8,128)(2,1)S(1)}, bf16[128,1024]{1,0:T(8,128)(2,1)}, bf16[128,1024]{1,0:T(8,128)(2,1)}, bf16[128,1024]{0,1:T(8,128)(2,1)S(1)}, bf16[128,1024]{0,1:T(8,128)(2,1)S(1)}) conditional(s32[]{:T(128)} %convert_element_type.118, () %tuple.77, (bf16[128,1024]{1,0:T(8,128)(2,1)S(1)}, bf16[1024,3072]{1,0:T(8,128)(2,1)}) %tuple.78), branch_computations={%region_5.5_spmd, %region_6.6_spmd} | conditional | flops 805699584 | bytes 9961512 | solution.py:123
  446.5 3.9 convolution_convert_fusion
  464.0 4.6 collective-permute-done.1
  469.9 13.0 %collective-permute-done.2 = bf16[128,1024]{0,1:T(8,128)(2,1)} collective-permute-done((bf16[128,1024]{0,1:T(8,128)(2,1)S(1)}, bf16[128,1024]{0,1:T(8,128)(2,1)}, u32[]{:S(2)}, u32[]{:S(2)}) %collective-permute-start.2) | collective-permute-done | bytes 262176 | tf_op jit(solution)/shard_map/while/body/eval_jaxpr/ppermute | solution.py:15
  482.9 5.5 %collective-permute-done.5 = bf16[128,1024]{0,1:T(8,128)(2,1)} collective-permute-done((bf16[128,1024]{0,1:T(8,128)(2,1)S(1)}, bf16[128,1024]{0,1:T(8,128)(2,1)}, u32[]{:S(2)}, u32[]{:S(2)}) %collective-permute-start.5) | collective-permute-done | bytes 262176 | tf_op jit(solution)/shard_map/while/body/eval_jaxpr/ppermute | solution.py:15
  488.4 17.1 %conditional.7 = (bf16[128,1024]{1,0:T(8,128)(2,1)}, f32[128,1024]{1,0:T(8,128)S(1)}, f32[128,1]{0,1:T(1,128)S(1)}) conditional(s32[]{:T(128)} %convert_element_type.118, () %tuple.76, (bf16[128,1024]{1,0:T(8,128)(2,1)S(1)}, bf16[128,1024]{1,0:T(8,128)(2,1)}, bf16[128,1024]{0,1:T(8,128)(2,1)}, bf16[128,1024]{0,1:T(8,128)(2,1)}, ...), branch_computations={%region_7.7_spmd, %region_8.12_spmd} | conditional | flops 1631453696 | bytes 34953780 | solution.py:130
  499.7 5.8 %multiply_reduce_fusion = (f32[128]{0:T(128)S(1)}, f32[128,1024]{1,0:T(8,128)S(1)}, bf16[128,1024]{1,0:T(8,128)(2,1)}) fusion(f32[128,1024]{1,0:T(8,128)S(1)} %get-tuple-element.364, bf16[2048,1024]{1,0:T(8,128)(2,1)} %get-tuple-element.201, bf16[1024,2048]{1,0:T(8,128)(2,1)} %get-tuple-element.200, f32[1024]{0:T(1024)S(1)} %bitcast.100, ...), kind=kOutput, calls=%fused_computation.38 | convolution fusion | flops 1077149568 | bytes 9704448 | tf_op jit(solution)/shard_map/while/body/eval_jaxpr/cond/branch_1_fun/dot_general | solution.py:107
  507.4 7.7 %collective-permute-done.6 = bf16[128,1024]{1,0:T(8,128)(2,1)S(1)} collective-permute-done((bf16[128,1024]{1,0:T(8,128)(2,1)}, bf16[128,1024]{1,0:T(8,128)(2,1)S(1)}, u32[]{:S(2)}, u32[]{:S(2)}) %collective-permute-start.6) | collective-permute-done | bytes 262176 | tf_op jit(solution)/shard_map/while/body/eval_jaxpr/ppermute | solution.py:15
  518.0 12.4 %all-reduce.1 = f32[8]{0:T(128)S(1)} all-reduce(f32[8]{0:T(128)S(1)} %bitcast_dynamic-update-slice_fusion), channel_id=2, replica_groups=mesh['section'=4,'ctx'=8] {'ctx'}, use_global_device_ids=true, to_apply=%add.1 | all-reduce | flops 8 | bytes 64 | tf_op jit(solution)/shard_map/all_gather | solution.py:153
  (305 shorter events, 194.8 us)
Async XLA Ops:
  11.3 10.8 %collective-permute-start = (bf16[128,1024]{0,1:T(8,128)(2,1)S(1)}, bf16[128,1024]{0,1:T(8,128)(2,1)S(1)}, u32[]{:S(2)}, u32[]{:S(2)}) collective-permute-start(bf16[128,1024]{0,1:T(8,128)(2,1)S(1)} %get-tuple-element.511), channel_id=1, source_target_pairs={{0,1},{1,2},{2,3},{3,4},{4,5},{5,6},{6,7},{8,9},{9,10},{10,11},{11... | collective-permute-start | bytes 786440 | tf_op jit(solution)/shard_map/while/body/eval_jaxpr/ppermute | solution.py:15
  15.0 10.7 %collective-permute-start.1 = (bf16[128,1024]{0,1:T(8,128)(2,1)S(1)}, bf16[128,1024]{0,1:T(8,128)(2,1)}, u32[]{:S(2)}, u32[]{:S(2)}) collective-permute-start(bf16[128,1024]{0,1:T(8,128)(2,1)S(1)} %get-tuple-element.511), channel_id=1, source_target_pairs={{0,2},{1,3},{2,4},{3,5},{4,6},{5,7},{8,10},{9,11},{10,12},{11,13},... | collective-permute-start | bytes 786440 | tf_op jit(solution)/shard_map/while/body/eval_jaxpr/ppermute | solution.py:15
  16.9 22.9 %collective-permute-start.2 = (bf16[128,1024]{0,1:T(8,128)(2,1)S(1)}, bf16[128,1024]{0,1:T(8,128)(2,1)}, u32[]{:S(2)}, u32[]{:S(2)}) collective-permute-start(bf16[128,1024]{0,1:T(8,128)(2,1)S(1)} %get-tuple-element.511), channel_id=1, source_target_pairs={{0,4},{1,5},{2,6},{3,7},{8,12},{9,13},{10,14},{11,15},{16,20},{17,... | collective-permute-start | bytes 786440 | tf_op jit(solution)/shard_map/while/body/eval_jaxpr/ppermute | solution.py:15
  18.2 21.6 %collective-permute-start.3 = (bf16[128,1024]{0,1:T(8,128)(2,1)S(1)}, bf16[128,1024]{0,1:T(8,128)(2,1)S(1)}, u32[]{:S(2)}, u32[]{:S(2)}) collective-permute-start(bf16[128,1024]{0,1:T(8,128)(2,1)S(1)} %get-tuple-element.513), channel_id=1, source_target_pairs={{0,1},{1,2},{2,3},{3,4},{4,5},{5,6},{6,7},{8,9},{9,10},{10,11},{11... | collective-permute-start | bytes 786440 | tf_op jit(solution)/shard_map/while/body/eval_jaxpr/ppermute | solution.py:15
  20.1 19.7 %collective-permute-start.4 = (bf16[128,1024]{0,1:T(8,128)(2,1)S(1)}, bf16[128,1024]{0,1:T(8,128)(2,1)}, u32[]{:S(2)}, u32[]{:S(2)}) collective-permute-start(bf16[128,1024]{0,1:T(8,128)(2,1)S(1)} %get-tuple-element.513), channel_id=1, source_target_pairs={{0,2},{1,3},{2,4},{3,5},{4,6},{5,7},{8,10},{9,11},{10,12},{11,13},... | collective-permute-start | bytes 786440 | tf_op jit(solution)/shard_map/while/body/eval_jaxpr/ppermute | solution.py:15
  22.1 23.4 %collective-permute-start.5 = (bf16[128,1024]{0,1:T(8,128)(2,1)S(1)}, bf16[128,1024]{0,1:T(8,128)(2,1)}, u32[]{:S(2)}, u32[]{:S(2)}) collective-permute-start(bf16[128,1024]{0,1:T(8,128)(2,1)S(1)} %get-tuple-element.513), channel_id=1, source_target_pairs={{0,4},{1,5},{2,6},{3,7},{8,12},{9,13},{10,14},{11,15},{16,20},{17,... | collective-permute-start | bytes 786440 | tf_op jit(solution)/shard_map/while/body/eval_jaxpr/ppermute | solution.py:15
  25.7 21.9 %collective-permute-start.7 = (f32[1,128]{1,0:T(1,128)S(1)}, f32[1,128]{1,0:T(1,128)S(1)}, u32[]{:S(2)}, u32[]{:S(2)}) collective-permute-start(f32[1,128]{1,0:T(1,128)S(1)} %broadcast_select_fusion.4), channel_id=1, source_target_pairs={{8,0},{16,8},{24,16},{9,1},{17,9},{25,17},{10,2},{18,10},{26,18},{... | collective-permute-start | bytes 1544 | tf_op jit(solution)/shard_map/while/body/eval_jaxpr/ppermute | solution.py:15
  64.4 13.1 %collective-permute-start.1 = (bf16[128,1024]{0,1:T(8,128)(2,1)S(1)}, bf16[128,1024]{0,1:T(8,128)(2,1)}, u32[]{:S(2)}, u32[]{:S(2)}) collective-permute-start(bf16[128,1024]{0,1:T(8,128)(2,1)S(1)} %get-tuple-element.511), channel_id=1, source_target_pairs={{0,2},{1,3},{2,4},{3,5},{4,6},{5,7},{8,10},{9,11},{10,12},{11,13},... | collective-permute-start | bytes 786440 | tf_op jit(solution)/shard_map/while/body/eval_jaxpr/ppermute | solution.py:15
  66.3 25.5 %collective-permute-start.2 = (bf16[128,1024]{0,1:T(8,128)(2,1)S(1)}, bf16[128,1024]{0,1:T(8,128)(2,1)}, u32[]{:S(2)}, u32[]{:S(2)}) collective-permute-start(bf16[128,1024]{0,1:T(8,128)(2,1)S(1)} %get-tuple-element.511), channel_id=1, source_target_pairs={{0,4},{1,5},{2,6},{3,7},{8,12},{9,13},{10,14},{11,15},{16,20},{17,... | collective-permute-start | bytes 786440 | tf_op jit(solution)/shard_map/while/body/eval_jaxpr/ppermute | solution.py:15
  67.6 24.2 %collective-permute-start.3 = (bf16[128,1024]{0,1:T(8,128)(2,1)S(1)}, bf16[128,1024]{0,1:T(8,128)(2,1)S(1)}, u32[]{:S(2)}, u32[]{:S(2)}) collective-permute-start(bf16[128,1024]{0,1:T(8,128)(2,1)S(1)} %get-tuple-element.513), channel_id=1, source_target_pairs={{0,1},{1,2},{2,3},{3,4},{4,5},{5,6},{6,7},{8,9},{9,10},{10,11},{11... | collective-permute-start | bytes 786440 | tf_op jit(solution)/shard_map/while/body/eval_jaxpr/ppermute | solution.py:15
  69.5 22.3 %collective-permute-start.4 = (bf16[128,1024]{0,1:T(8,128)(2,1)S(1)}, bf16[128,1024]{0,1:T(8,128)(2,1)}, u32[]{:S(2)}, u32[]{:S(2)}) collective-permute-start(bf16[128,1024]{0,1:T(8,128)(2,1)S(1)} %get-tuple-element.513), channel_id=1, source_target_pairs={{0,2},{1,3},{2,4},{3,5},{4,6},{5,7},{8,10},{9,11},{10,12},{11,13},... | collective-permute-start | bytes 786440 | tf_op jit(solution)/shard_map/while/body/eval_jaxpr/ppermute | solution.py:15
  71.5 25.8 %collective-permute-start.5 = (bf16[128,1024]{0,1:T(8,128)(2,1)S(1)}, bf16[128,1024]{0,1:T(8,128)(2,1)}, u32[]{:S(2)}, u32[]{:S(2)}) collective-permute-start(bf16[128,1024]{0,1:T(8,128)(2,1)S(1)} %get-tuple-element.513), channel_id=1, source_target_pairs={{0,4},{1,5},{2,6},{3,7},{8,12},{9,13},{10,14},{11,15},{16,20},{17,... | collective-permute-start | bytes 786440 | tf_op jit(solution)/shard_map/while/body/eval_jaxpr/ppermute | solution.py:15
  77.5 21.9 %collective-permute-start.7 = (f32[1,128]{1,0:T(1,128)S(1)}, f32[1,128]{1,0:T(1,128)S(1)}, u32[]{:S(2)}, u32[]{:S(2)}) collective-permute-start(f32[1,128]{1,0:T(1,128)S(1)} %broadcast_select_fusion.4), channel_id=1, source_target_pairs={{8,0},{16,8},{24,16},{9,1},{17,9},{25,17},{10,2},{18,10},{26,18},{... | collective-permute-start | bytes 1544 | tf_op jit(solution)/shard_map/while/body/eval_jaxpr/ppermute | solution.py:15
  98.1 16.0 %collective-permute-start.6 = (bf16[128,1024]{1,0:T(8,128)(2,1)}, bf16[128,1024]{1,0:T(8,128)(2,1)S(1)}, u32[]{:S(2)}, u32[]{:S(2)}) collective-permute-start(bf16[128,1024]{1,0:T(8,128)(2,1)} %get-tuple-element.515), channel_id=1, source_target_pairs={{0,8},{8,16},{16,24},{1,9},{9,17},{17,25},{2,10},{10,18},{18,26},{... | collective-permute-start | bytes 786440 | tf_op jit(solution)/shard_map/while/body/eval_jaxpr/ppermute | solution.py:15
  122.7 13.1 %collective-permute-start.1 = (bf16[128,1024]{0,1:T(8,128)(2,1)S(1)}, bf16[128,1024]{0,1:T(8,128)(2,1)}, u32[]{:S(2)}, u32[]{:S(2)}) collective-permute-start(bf16[128,1024]{0,1:T(8,128)(2,1)S(1)} %get-tuple-element.511), channel_id=1, source_target_pairs={{0,2},{1,3},{2,4},{3,5},{4,6},{5,7},{8,10},{9,11},{10,12},{11,13},... | collective-permute-start | bytes 786440 | tf_op jit(solution)/shard_map/while/body/eval_jaxpr/ppermute | solution.py:15
  124.6 52.7 %collective-permute-start.2 = (bf16[128,1024]{0,1:T(8,128)(2,1)S(1)}, bf16[128,1024]{0,1:T(8,128)(2,1)}, u32[]{:S(2)}, u32[]{:S(2)}) collective-permute-start(bf16[128,1024]{0,1:T(8,128)(2,1)S(1)} %get-tuple-element.511), channel_id=1, source_target_pairs={{0,4},{1,5},{2,6},{3,7},{8,12},{9,13},{10,14},{11,15},{16,20},{17,... | collective-permute-start | bytes 786440 | tf_op jit(solution)/shard_map/while/body/eval_jaxpr/ppermute | solution.py:15
  125.9 51.4 %collective-permute-start.3 = (bf16[128,1024]{0,1:T(8,128)(2,1)S(1)}, bf16[128,1024]{0,1:T(8,128)(2,1)S(1)}, u32[]{:S(2)}, u32[]{:S(2)}) collective-permute-start(bf16[128,1024]{0,1:T(8,128)(2,1)S(1)} %get-tuple-element.513), channel_id=1, source_target_pairs={{0,1},{1,2},{2,3},{3,4},{4,5},{5,6},{6,7},{8,9},{9,10},{10,11},{11... | collective-permute-start | bytes 786440 | tf_op jit(solution)/shard_map/while/body/eval_jaxpr/ppermute | solution.py:15
  127.8 49.5 %collective-permute-start.4 = (bf16[128,1024]{0,1:T(8,128)(2,1)S(1)}, bf16[128,1024]{0,1:T(8,128)(2,1)}, u32[]{:S(2)}, u32[]{:S(2)}) collective-permute-start(bf16[128,1024]{0,1:T(8,128)(2,1)S(1)} %get-tuple-element.513), channel_id=1, source_target_pairs={{0,2},{1,3},{2,4},{3,5},{4,6},{5,7},{8,10},{9,11},{10,12},{11,13},... | collective-permute-start | bytes 786440 | tf_op jit(solution)/shard_map/while/body/eval_jaxpr/ppermute | solution.py:15
  129.8 47.6 %collective-permute-start.5 = (bf16[128,1024]{0,1:T(8,128)(2,1)S(1)}, bf16[128,1024]{0,1:T(8,128)(2,1)}, u32[]{:S(2)}, u32[]{:S(2)}) collective-permute-start(bf16[128,1024]{0,1:T(8,128)(2,1)S(1)} %get-tuple-element.513), channel_id=1, source_target_pairs={{0,4},{1,5},{2,6},{3,7},{8,12},{9,13},{10,14},{11,15},{16,20},{17,... | collective-permute-start | bytes 786440 | tf_op jit(solution)/shard_map/while/body/eval_jaxpr/ppermute | solution.py:15
  135.8 43.7 %collective-permute-start.7 = (f32[1,128]{1,0:T(1,128)S(1)}, f32[1,128]{1,0:T(1,128)S(1)}, u32[]{:S(2)}, u32[]{:S(2)}) collective-permute-start(f32[1,128]{1,0:T(1,128)S(1)} %broadcast_select_fusion.4), channel_id=1, source_target_pairs={{8,0},{16,8},{24,16},{9,1},{17,9},{25,17},{10,2},{18,10},{26,18},{... | collective-permute-start | bytes 1544 | tf_op jit(solution)/shard_map/while/body/eval_jaxpr/ppermute | solution.py:15
  178.2 42.6 %collective-permute-start.6 = (bf16[128,1024]{1,0:T(8,128)(2,1)}, bf16[128,1024]{1,0:T(8,128)(2,1)S(1)}, u32[]{:S(2)}, u32[]{:S(2)}) collective-permute-start(bf16[128,1024]{1,0:T(8,128)(2,1)} %get-tuple-element.515), channel_id=1, source_target_pairs={{0,8},{8,16},{16,24},{1,9},{9,17},{17,25},{2,10},{10,18},{18,26},{... | collective-permute-start | bytes 786440 | tf_op jit(solution)/shard_map/while/body/eval_jaxpr/ppermute | solution.py:15
  234.9 12.7 %collective-permute-start.1 = (bf16[128,1024]{0,1:T(8,128)(2,1)S(1)}, bf16[128,1024]{0,1:T(8,128)(2,1)}, u32[]{:S(2)}, u32[]{:S(2)}) collective-permute-start(bf16[128,1024]{0,1:T(8,128)(2,1)S(1)} %get-tuple-element.511), channel_id=1, source_target_pairs={{0,2},{1,3},{2,4},{3,5},{4,6},{5,7},{8,10},{9,11},{10,12},{11,13},... | collective-permute-start | bytes 786440 | tf_op jit(solution)/shard_map/while/body/eval_jaxpr/ppermute | solution.py:15
  236.9 25.1 %collective-permute-start.2 = (bf16[128,1024]{0,1:T(8,128)(2,1)S(1)}, bf16[128,1024]{0,1:T(8,128)(2,1)}, u32[]{:S(2)}, u32[]{:S(2)}) collective-permute-start(bf16[128,1024]{0,1:T(8,128)(2,1)S(1)} %get-tuple-element.511), channel_id=1, source_target_pairs={{0,4},{1,5},{2,6},{3,7},{8,12},{9,13},{10,14},{11,15},{16,20},{17,... | collective-permute-start | bytes 786440 | tf_op jit(solution)/shard_map/while/body/eval_jaxpr/ppermute | solution.py:15
  238.2 23.8 %collective-permute-start.3 = (bf16[128,1024]{0,1:T(8,128)(2,1)S(1)}, bf16[128,1024]{0,1:T(8,128)(2,1)S(1)}, u32[]{:S(2)}, u32[]{:S(2)}) collective-permute-start(bf16[128,1024]{0,1:T(8,128)(2,1)S(1)} %get-tuple-element.513), channel_id=1, source_target_pairs={{0,1},{1,2},{2,3},{3,4},{4,5},{5,6},{6,7},{8,9},{9,10},{10,11},{11... | collective-permute-start | bytes 786440 | tf_op jit(solution)/shard_map/while/body/eval_jaxpr/ppermute | solution.py:15
  240.1 21.8 %collective-permute-start.4 = (bf16[128,1024]{0,1:T(8,128)(2,1)S(1)}, bf16[128,1024]{0,1:T(8,128)(2,1)}, u32[]{:S(2)}, u32[]{:S(2)}) collective-permute-start(bf16[128,1024]{0,1:T(8,128)(2,1)S(1)} %get-tuple-element.513), channel_id=1, source_target_pairs={{0,2},{1,3},{2,4},{3,5},{4,6},{5,7},{8,10},{9,11},{10,12},{11,13},... | collective-permute-start | bytes 786440 | tf_op jit(solution)/shard_map/while/body/eval_jaxpr/ppermute | solution.py:15
  242.0 25.4 %collective-permute-start.5 = (bf16[128,1024]{0,1:T(8,128)(2,1)S(1)}, bf16[128,1024]{0,1:T(8,128)(2,1)}, u32[]{:S(2)}, u32[]{:S(2)}) collective-permute-start(bf16[128,1024]{0,1:T(8,128)(2,1)S(1)} %get-tuple-element.513), channel_id=1, source_target_pairs={{0,4},{1,5},{2,6},{3,7},{8,12},{9,13},{10,14},{11,15},{16,20},{17,... | collective-permute-start | bytes 786440 | tf_op jit(solution)/shard_map/while/body/eval_jaxpr/ppermute | solution.py:15
  247.6 38.2 %collective-permute-start.7 = (f32[1,128]{1,0:T(1,128)S(1)}, f32[1,128]{1,0:T(1,128)S(1)}, u32[]{:S(2)}, u32[]{:S(2)}) collective-permute-start(f32[1,128]{1,0:T(1,128)S(1)} %broadcast_select_fusion.4), channel_id=1, source_target_pairs={{8,0},{16,8},{24,16},{9,1},{17,9},{25,17},{10,2},{18,10},{26,18},{... | collective-permute-start | bytes 1544 | tf_op jit(solution)/shard_map/while/body/eval_jaxpr/ppermute | solution.py:15
  284.6 9.6 %collective-permute-start.6 = (bf16[128,1024]{1,0:T(8,128)(2,1)}, bf16[128,1024]{1,0:T(8,128)(2,1)S(1)}, u32[]{:S(2)}, u32[]{:S(2)}) collective-permute-start(bf16[128,1024]{1,0:T(8,128)(2,1)} %get-tuple-element.515), channel_id=1, source_target_pairs={{0,8},{8,16},{16,24},{1,9},{9,17},{17,25},{2,10},{10,18},{18,26},{... | collective-permute-start | bytes 786440 | tf_op jit(solution)/shard_map/while/body/eval_jaxpr/ppermute | solution.py:15
  308.2 13.0 %collective-permute-start.1 = (bf16[128,1024]{0,1:T(8,128)(2,1)S(1)}, bf16[128,1024]{0,1:T(8,128)(2,1)}, u32[]{:S(2)}, u32[]{:S(2)}) collective-permute-start(bf16[128,1024]{0,1:T(8,128)(2,1)S(1)} %get-tuple-element.511), channel_id=1, source_target_pairs={{0,2},{1,3},{2,4},{3,5},{4,6},{5,7},{8,10},{9,11},{10,12},{11,13},... | collective-permute-start | bytes 786440 | tf_op jit(solution)/shard_map/while/body/eval_jaxpr/ppermute | solution.py:15
  310.2 25.4 %collective-permute-start.2 = (bf16[128,1024]{0,1:T(8,128)(2,1)S(1)}, bf16[128,1024]{0,1:T(8,128)(2,1)}, u32[]{:S(2)}, u32[]{:S(2)}) collective-permute-start(bf16[128,1024]{0,1:T(8,128)(2,1)S(1)} %get-tuple-element.511), channel_id=1, source_target_pairs={{0,4},{1,5},{2,6},{3,7},{8,12},{9,13},{10,14},{11,15},{16,20},{17,... | collective-permute-start | bytes 786440 | tf_op jit(solution)/shard_map/while/body/eval_jaxpr/ppermute | solution.py:15
  311.5 24.1 %collective-permute-start.3 = (bf16[128,1024]{0,1:T(8,128)(2,1)S(1)}, bf16[128,1024]{0,1:T(8,128)(2,1)S(1)}, u32[]{:S(2)}, u32[]{:S(2)}) collective-permute-start(bf16[128,1024]{0,1:T(8,128)(2,1)S(1)} %get-tuple-element.513), channel_id=1, source_target_pairs={{0,1},{1,2},{2,3},{3,4},{4,5},{5,6},{6,7},{8,9},{9,10},{10,11},{11... | collective-permute-start | bytes 786440 | tf_op jit(solution)/shard_map/while/body/eval_jaxpr/ppermute | solution.py:15
  313.4 22.2 %collective-permute-start.4 = (bf16[128,1024]{0,1:T(8,128)(2,1)S(1)}, bf16[128,1024]{0,1:T(8,128)(2,1)}, u32[]{:S(2)}, u32[]{:S(2)}) collective-permute-start(bf16[128,1024]{0,1:T(8,128)(2,1)S(1)} %get-tuple-element.513), channel_id=1, source_target_pairs={{0,2},{1,3},{2,4},{3,5},{4,6},{5,7},{8,10},{9,11},{10,12},{11,13},... | collective-permute-start | bytes 786440 | tf_op jit(solution)/shard_map/while/body/eval_jaxpr/ppermute | solution.py:15
  315.4 25.7 %collective-permute-start.5 = (bf16[128,1024]{0,1:T(8,128)(2,1)S(1)}, bf16[128,1024]{0,1:T(8,128)(2,1)}, u32[]{:S(2)}, u32[]{:S(2)}) collective-permute-start(bf16[128,1024]{0,1:T(8,128)(2,1)S(1)} %get-tuple-element.513), channel_id=1, source_target_pairs={{0,4},{1,5},{2,6},{3,7},{8,12},{9,13},{10,14},{11,15},{16,20},{17,... | collective-permute-start | bytes 786440 | tf_op jit(solution)/shard_map/while/body/eval_jaxpr/ppermute | solution.py:15
  321.3 38.2 %collective-permute-start.7 = (f32[1,128]{1,0:T(1,128)S(1)}, f32[1,128]{1,0:T(1,128)S(1)}, u32[]{:S(2)}, u32[]{:S(2)}) collective-permute-start(f32[1,128]{1,0:T(1,128)S(1)} %broadcast_select_fusion.4), channel_id=1, source_target_pairs={{8,0},{16,8},{24,16},{9,1},{17,9},{25,17},{10,2},{18,10},{26,18},{... | collective-permute-start | bytes 1544 | tf_op jit(solution)/shard_map/while/body/eval_jaxpr/ppermute | solution.py:15
  358.2 9.6 %collective-permute-start.6 = (bf16[128,1024]{1,0:T(8,128)(2,1)}, bf16[128,1024]{1,0:T(8,128)(2,1)S(1)}, u32[]{:S(2)}, u32[]{:S(2)}) collective-permute-start(bf16[128,1024]{1,0:T(8,128)(2,1)} %get-tuple-element.515), channel_id=1, source_target_pairs={{0,8},{8,16},{16,24},{1,9},{9,17},{17,25},{2,10},{10,18},{18,26},{... | collective-permute-start | bytes 786440 | tf_op jit(solution)/shard_map/while/body/eval_jaxpr/ppermute | solution.py:15
  381.9 13.0 %collective-permute-start.1 = (bf16[128,1024]{0,1:T(8,128)(2,1)S(1)}, bf16[128,1024]{0,1:T(8,128)(2,1)}, u32[]{:S(2)}, u32[]{:S(2)}) collective-permute-start(bf16[128,1024]{0,1:T(8,128)(2,1)S(1)} %get-tuple-element.511), channel_id=1, source_target_pairs={{0,2},{1,3},{2,4},{3,5},{4,6},{5,7},{8,10},{9,11},{10,12},{11,13},... | collective-permute-start | bytes 786440 | tf_op jit(solution)/shard_map/while/body/eval_jaxpr/ppermute | solution.py:15
  383.8 25.4 %collective-permute-start.2 = (bf16[128,1024]{0,1:T(8,128)(2,1)S(1)}, bf16[128,1024]{0,1:T(8,128)(2,1)}, u32[]{:S(2)}, u32[]{:S(2)}) collective-permute-start(bf16[128,1024]{0,1:T(8,128)(2,1)S(1)} %get-tuple-element.511), channel_id=1, source_target_pairs={{0,4},{1,5},{2,6},{3,7},{8,12},{9,13},{10,14},{11,15},{16,20},{17,... | collective-permute-start | bytes 786440 | tf_op jit(solution)/shard_map/while/body/eval_jaxpr/ppermute | solution.py:15
  385.1 24.1 %collective-permute-start.3 = (bf16[128,1024]{0,1:T(8,128)(2,1)S(1)}, bf16[128,1024]{0,1:T(8,128)(2,1)S(1)}, u32[]{:S(2)}, u32[]{:S(2)}) collective-permute-start(bf16[128,1024]{0,1:T(8,128)(2,1)S(1)} %get-tuple-element.513), channel_id=1, source_target_pairs={{0,1},{1,2},{2,3},{3,4},{4,5},{5,6},{6,7},{8,9},{9,10},{10,11},{11... | collective-permute-start | bytes 786440 | tf_op jit(solution)/shard_map/while/body/eval_jaxpr/ppermute | solution.py:15
  387.1 22.2 %collective-permute-start.4 = (bf16[128,1024]{0,1:T(8,128)(2,1)S(1)}, bf16[128,1024]{0,1:T(8,128)(2,1)}, u32[]{:S(2)}, u32[]{:S(2)}) collective-permute-start(bf16[128,1024]{0,1:T(8,128)(2,1)S(1)} %get-tuple-element.513), channel_id=1, source_target_pairs={{0,2},{1,3},{2,4},{3,5},{4,6},{5,7},{8,10},{9,11},{10,12},{11,13},... | collective-permute-start | bytes 786440 | tf_op jit(solution)/shard_map/while/body/eval_jaxpr/ppermute | solution.py:15
  389.0 25.7 %collective-permute-start.5 = (bf16[128,1024]{0,1:T(8,128)(2,1)S(1)}, bf16[128,1024]{0,1:T(8,128)(2,1)}, u32[]{:S(2)}, u32[]{:S(2)}) collective-permute-start(bf16[128,1024]{0,1:T(8,128)(2,1)S(1)} %get-tuple-element.513), channel_id=1, source_target_pairs={{0,4},{1,5},{2,6},{3,7},{8,12},{9,13},{10,14},{11,15},{16,20},{17,... | collective-permute-start | bytes 786440 | tf_op jit(solution)/shard_map/while/body/eval_jaxpr/ppermute | solution.py:15
  394.9 38.2 %collective-permute-start.7 = (f32[1,128]{1,0:T(1,128)S(1)}, f32[1,128]{1,0:T(1,128)S(1)}, u32[]{:S(2)}, u32[]{:S(2)}) collective-permute-start(f32[1,128]{1,0:T(1,128)S(1)} %broadcast_select_fusion.4), channel_id=1, source_target_pairs={{8,0},{16,8},{24,16},{9,1},{17,9},{25,17},{10,2},{18,10},{26,18},{... | collective-permute-start | bytes 1544 | tf_op jit(solution)/shard_map/while/body/eval_jaxpr/ppermute | solution.py:15
  431.9 9.6 %collective-permute-start.6 = (bf16[128,1024]{1,0:T(8,128)(2,1)}, bf16[128,1024]{1,0:T(8,128)(2,1)S(1)}, u32[]{:S(2)}, u32[]{:S(2)}) collective-permute-start(bf16[128,1024]{1,0:T(8,128)(2,1)} %get-tuple-element.515), channel_id=1, source_target_pairs={{0,8},{8,16},{16,24},{1,9},{9,17},{17,25},{2,10},{10,18},{18,26},{... | collective-permute-start | bytes 786440 | tf_op jit(solution)/shard_map/while/body/eval_jaxpr/ppermute | solution.py:15
  455.5 13.0 %collective-permute-start.1 = (bf16[128,1024]{0,1:T(8,128)(2,1)S(1)}, bf16[128,1024]{0,1:T(8,128)(2,1)}, u32[]{:S(2)}, u32[]{:S(2)}) collective-permute-start(bf16[128,1024]{0,1:T(8,128)(2,1)S(1)} %get-tuple-element.511), channel_id=1, source_target_pairs={{0,2},{1,3},{2,4},{3,5},{4,6},{5,7},{8,10},{9,11},{10,12},{11,13},... | collective-permute-start | bytes 786440 | tf_op jit(solution)/shard_map/while/body/eval_jaxpr/ppermute | solution.py:15
  457.5 25.4 %collective-permute-start.2 = (bf16[128,1024]{0,1:T(8,128)(2,1)S(1)}, bf16[128,1024]{0,1:T(8,128)(2,1)}, u32[]{:S(2)}, u32[]{:S(2)}) collective-permute-start(bf16[128,1024]{0,1:T(8,128)(2,1)S(1)} %get-tuple-element.511), channel_id=1, source_target_pairs={{0,4},{1,5},{2,6},{3,7},{8,12},{9,13},{10,14},{11,15},{16,20},{17,... | collective-permute-start | bytes 786440 | tf_op jit(solution)/shard_map/while/body/eval_jaxpr/ppermute | solution.py:15
  458.8 24.1 %collective-permute-start.3 = (bf16[128,1024]{0,1:T(8,128)(2,1)S(1)}, bf16[128,1024]{0,1:T(8,128)(2,1)S(1)}, u32[]{:S(2)}, u32[]{:S(2)}) collective-permute-start(bf16[128,1024]{0,1:T(8,128)(2,1)S(1)} %get-tuple-element.513), channel_id=1, source_target_pairs={{0,1},{1,2},{2,3},{3,4},{4,5},{5,6},{6,7},{8,9},{9,10},{10,11},{11... | collective-permute-start | bytes 786440 | tf_op jit(solution)/shard_map/while/body/eval_jaxpr/ppermute | solution.py:15
  460.7 22.2 %collective-permute-start.4 = (bf16[128,1024]{0,1:T(8,128)(2,1)S(1)}, bf16[128,1024]{0,1:T(8,128)(2,1)}, u32[]{:S(2)}, u32[]{:S(2)}) collective-permute-start(bf16[128,1024]{0,1:T(8,128)(2,1)S(1)} %get-tuple-element.513), channel_id=1, source_target_pairs={{0,2},{1,3},{2,4},{3,5},{4,6},{5,7},{8,10},{9,11},{10,12},{11,13},... | collective-permute-start | bytes 786440 | tf_op jit(solution)/shard_map/while/body/eval_jaxpr/ppermute | solution.py:15
  462.7 25.7 %collective-permute-start.5 = (bf16[128,1024]{0,1:T(8,128)(2,1)S(1)}, bf16[128,1024]{0,1:T(8,128)(2,1)}, u32[]{:S(2)}, u32[]{:S(2)}) collective-permute-start(bf16[128,1024]{0,1:T(8,128)(2,1)S(1)} %get-tuple-element.513), channel_id=1, source_target_pairs={{0,4},{1,5},{2,6},{3,7},{8,12},{9,13},{10,14},{11,15},{16,20},{17,... | collective-permute-start | bytes 786440 | tf_op jit(solution)/shard_map/while/body/eval_jaxpr/ppermute | solution.py:15
  468.6 38.2 %collective-permute-start.7 = (f32[1,128]{1,0:T(1,128)S(1)}, f32[1,128]{1,0:T(1,128)S(1)}, u32[]{:S(2)}, u32[]{:S(2)}) collective-permute-start(f32[1,128]{1,0:T(1,128)S(1)} %broadcast_select_fusion.4), channel_id=1, source_target_pairs={{8,0},{16,8},{24,16},{9,1},{17,9},{25,17},{10,2},{18,10},{26,18},{... | collective-permute-start | bytes 1544 | tf_op jit(solution)/shard_map/while/body/eval_jaxpr/ppermute | solution.py:15
  (41 other events, 1288.4 us)
where the time goes:
time: 536 us; the launch traced here: 532 us
  waiting for transfers between devices  226 us (42%)
  starting transfers between devices  140 us (26%)
  matrix products  64 us (12%)
  local copies, waits for them, and re-layouts  43.4 us (8%)
  other arithmetic  33.3 us (6%)
  blocking collectives  12.4 us (2%)
  loops' own time  11.8 us (2%)
    ppermute x56, waiting for transfers between devices, from_behind(): return lax.ppermute(value, axis, pairs)  226 us
    ppermute x56, starting transfers between devices, from_behind(): return lax.ppermute(value, axis, pairs)  140 us
    dot_general x4, matrix products, finish(): jnp.dot(activated, weight_down, preferred_element_type=jnp.float32)  23.2 us
    dot_general x4, matrix products, project(): jnp.dot(normed_rows, weight_qkv, preferred_element_type=jnp.float32)  15.7 us
    sub x4, other arithmetic, finish(): weights = jax.nn.softmax(scores, axis=-1).astype(jnp.bfloat16)  14.5 us
    all_gather x1, blocking collectives, body(): lax.all_gather(totals, 'ctx', axis=0, tiled=True)  12.4 us
    dot_general x4, matrix products, finish(): jnp.einsum('shqk,skhd->sqhd', weights, value_all, preferred_element_type=...  11.4 us
    another operation x1, loops' own time, body(): lax.scan(section_step, initial, jnp.arange(tick_count, dtype=jnp.int32))  11.2 us
  transfers between devices with their start and end apart: 56, of which 26 were waited for; matrix products, arithmetic and copies ran while one was open for 14% of the time, Pallas kernels for 0%

commit v1 on v0

v1 whole, which is shorter than its diff:
```python
import functools
import math

import jax
import jax.numpy as jnp
from jax import lax
from jax.experimental import pallas as pl
from jax.experimental.pallas import tpu as pltpu
from jax.sharding import PartitionSpec as P

HEADS = 16
NDIL = 3
CORES = 2
LANES = 128
PARTS = 2
MASKED = -1e30


def rms_normed(vector):
    return vector * lax.rsqrt(jnp.mean(vector * vector, axis=-1, keepdims=True) + 1e-05)


def kernel(
    sections,
    ctx_count,
    spins_ref,
    mask_ref,
    tok_ref,
    pos_hbm,
    gain1_ref,
    wqkv_hbm,
    wout_hbm,
    gain2_ref,
    wup_hbm,
    wdown_hbm,
    whead_ref,
    out_ref,
    wqkv,
    wout,
    wup,
    wdown,
    pos,
    xin,
    xout,
    kv_own,
    kv_far,
    queries,
    attended,
    activated,
    hidden,
    bias,
    mask_send,
    mask_rows,
    totals_send,
    totals_far,
    rows_keep,
    result_send,
    result_in,
    w_sem,
    pos_local_sem,
    pos_send_sem,
    pos_recv_sem,
    mask_send_sem,
    mask_recv_sem,
    x_send_sem,
    x_recv_sem,
    kv_send_sem,
    kv_recv_sem,
    tot_send_sem,
    tot_recv_sem,
    res_send_sem,
    res_recv_sem,
):
    ticks = ctx_count // CORES
    groups = ticks
    block_len, width = pos.shape[1], pos.shape[2]
    part_width = width // PARTS
    hid = wup.shape[1]
    head_dim = width // HEADS
    s = lax.axis_index("section")
    b = lax.axis_index("ctx")
    n = b // CORES
    c = b % CORES
    partner = b + 1 - 2 * c
    last = sections - 1

    def ring(step):
        return lax.rem(n + step, groups)

    w_copies = [
        pltpu.make_async_copy(wqkv_hbm.at[0], wqkv, w_sem.at[0]),
        pltpu.make_async_copy(wout_hbm.at[0], wout, w_sem.at[1]),
        pltpu.make_async_copy(wup_hbm.at[0], wup, w_sem.at[2]),
        pltpu.make_async_copy(wdown_hbm.at[0], wdown, w_sem.at[3]),
    ]
    pos_local = pltpu.make_async_copy(pos_hbm, pos.at[n], pos_local_sem)

    @pl.when(s == 0)
    def _():
        pos_local.start()

    for copy in w_copies:
        copy.start()

    barrier = pltpu.get_barrier_semaphore()

    def greet(section, ctx):
        pl.semaphore_signal(
            barrier, inc=1, device_id=(section, ctx), device_id_type=pl.DeviceIdType.MESH
        )

    greet(s, partner)
    for step in range(1, groups):
        greet(s, ring(step) * CORES + c)

    @pl.when(s > 0)
    def _():
        greet(s - 1, b)

    result_from = s * CORES + c
    from_self = (s == last) & (b == result_from)

    @pl.when(jnp.logical_not(from_self))
    def _():
        greet(last, result_from)

    lane = lax.broadcasted_iota(jnp.int32, (8, LANES), 1)
    mask_send[...] = jnp.zeros((8, LANES), jnp.float32)
    mask_send[0:1, 0:ctx_count] = mask_ref[...].astype(jnp.float32)
    mask_rows[n] = mask_send[...]

    blank = jnp.zeros((block_len, 2 * width), jnp.bfloat16)
    for slot in range(1 << (NDIL - 2)):
        kv_own[slot] = blank
    kv_far[0] = blank

    receivers = groups + jnp.where(
        s < last, 1, ticks - jnp.where(n == last, 1, 0)
    )
    pl.semaphore_wait(barrier, receivers)

    def remote(src, dst, send_sem, recv_sem, section, ctx):
        return pltpu.make_async_remote_copy(
            src_ref=src,
            dst_ref=dst,
            send_sem=send_sem,
            recv_sem=recv_sem,
            device_id=(section, ctx),
            device_id_type=pl.DeviceIdType.MESH,
        )

    def mask_copy(step):
        return remote(
            mask_send, mask_rows.at[n], mask_send_sem.at[step], mask_recv_sem.at[n],
            s, ring(step) * CORES + c,
        )

    def pos_copy(step):
        return remote(
            pos_hbm, pos.at[n], pos_send_sem.at[step], pos_recv_sem.at[n],
            0, ring(step) * CORES + c,
        )

    for step in range(1, groups):
        mask_copy(step).start()

    @pl.when(s == 0)
    def _():
        for step in range(1, groups):
            pos_copy(step).start()

    def mask_arrival(slot):
        return remote(
            mask_send, mask_rows.at[slot], mask_send_sem.at[0], mask_recv_sem.at[slot], s, partner
        )

    def pos_arrival(slot):
        return remote(pos_hbm, pos.at[slot], pos_send_sem.at[0], pos_recv_sem.at[slot], 0, partner)

    def x_copy(j, part):
        return remote(
            xout.at[j, part], xin.at[j, part], x_send_sem.at[j, part], x_recv_sem.at[j, part],
            s + 1, b,
        )

    def kv_copy(j):
        return remote(
            kv_own.at[j + (1 << (NDIL - 2))], kv_far.at[j + 1], kv_send_sem.at[j],
            kv_recv_sem.at[j + 1], s, partner,
        )

    def kv_arrival(slot):
        return remote(
            kv_far.at[slot], kv_far.at[slot], kv_send_sem.at[0], kv_recv_sem.at[slot], s, partner
        )

    def total_copy(j):
        return remote(
            totals_send.at[j], totals_far.at[j], tot_send_sem.at[j], tot_recv_sem.at[j], s, partner
        )

    row_at = lax.broadcasted_iota(jnp.int32, (block_len, block_len), 0)
    col_at = lax.broadcasted_iota(jnp.int32, (block_len, block_len), 1)

    def spins_row(block):
        at = pl.multiple_of(block * block_len, block_len)
        rows = spins_ref[:, pl.ds(at, block_len)].astype(jnp.float32)
        which = lax.broadcasted_iota(jnp.int32, rows.shape, 0)
        return jnp.sum(jnp.where(which == n, rows, 0.0), axis=0, keepdims=True)

    def tick(j, carry):
        block = j * CORES + c

        @pl.when(j != n)
        def _():
            mask_arrival(j).wait_recv()

        flags = mask_rows[j]
        bias[:, 0:block_len] = jnp.where(col_at <= row_at, 0.0, MASKED)
        for level in range(NDIL):
            source = block - (1 << level)
            hit = jnp.where((lane == source) & (flags > 0.5), 1.0, 0.0)
            hit = jnp.sum(hit[0:1], axis=1, keepdims=True)
            bias[:, (level + 1) * block_len : (level + 2) * block_len] = jnp.broadcast_to(
                jnp.where(hit > 0.5, 0.0, MASKED), (block_len, block_len)
            )

        @pl.when(s == 0)
        def _():
            @pl.when(j == n)
            def _():
                pos_local.wait()

            @pl.when(j != n)
            def _():
                pos_arrival(j).wait_recv()

            row = spins_row(block)
            before = spins_row(jnp.maximum(block - 1, 0))[:, block_len - 1 : block_len]
            first = jnp.where(block > 0, before, 2.0)
            token = jnp.sum(jnp.where(col_at == row_at - 1, row, 0.0), axis=1, keepdims=True)
            token = jnp.where(row_at[:, 0:1] == 0, first, token)
            rows = jnp.where(
                token == 0.0,
                tok_ref[0:1, :],
                jnp.where(token == 1.0, tok_ref[1:2, :], tok_ref[2:3, :]),
            )
            rows = (rows + pos[j].astype(jnp.float32)).astype(jnp.bfloat16)
            for part in range(PARTS):
                xin[j, part] = rows[:, part * part_width : (part + 1) * part_width]

        @pl.when(s > 0)
        def _():
            for part in range(PARTS):
                remote(
                    xout.at[j, part], xin.at[j, part], x_send_sem.at[j, part],
                    x_recv_sem.at[j, part], s, partner,
                ).wait_recv()

        layer_in = jnp.concatenate([xin[j, part] for part in range(PARTS)], axis=1)
        layer_in = layer_in.astype(jnp.float32)
        hidden[...] = layer_in
        normed = (rms_normed(layer_in) * gain1_ref[...]).astype(jnp.bfloat16)

        @pl.when(j == 0)
        def _():
            w_copies[0].wait()

        own = j + (1 << (NDIL - 2))
        for chunk in range(width, 3 * width, 512):
            kv_own[own, :, chunk - width : chunk - width + 512] = jnp.dot(
                normed, wqkv[:, chunk : chunk + 512], preferred_element_type=jnp.float32
            ).astype(jnp.bfloat16)

        @pl.when((c == 0) | (j < ticks - 1))
        def _():
            kv_copy(j).start()

        for chunk in range(0, width, 512):
            queries[:, chunk : chunk + 512] = (
                jnp.dot(normed, wqkv[:, chunk : chunk + 512], preferred_element_type=jnp.float32)
                .astype(jnp.bfloat16)
                .astype(jnp.float32)
                * (1.0 / math.sqrt(head_dim))
            ).astype(jnp.bfloat16)

        @pl.when(j + c > 0)
        def _():
            kv_arrival(j + c).wait_recv()

        key_slots = [(kv_own, own), (kv_far, j + c)]
        for level in range(1, NDIL):
            key_slots.append((kv_own, own - (1 << (level - 1))))
        bias_two = jnp.concatenate([bias[...], bias[...]], axis=0)
        lane_low = lax.broadcasted_iota(jnp.int32, (block_len, LANES), 1) < head_dim
        for pair in range(width // LANES):
            cols = slice(pair * LANES, (pair + 1) * LANES)
            vcols = slice(width + pair * LANES, width + (pair + 1) * LANES)
            q_pair = queries[:, cols]
            zero = jnp.zeros_like(q_pair)
            q_two = jnp.concatenate(
                [jnp.where(lane_low, q_pair, zero), jnp.where(lane_low, zero, q_pair)], axis=0
            )
            keys = jnp.concatenate([ref[at, :, cols] for ref, at in key_slots], axis=0)
            values = jnp.concatenate([ref[at, :, vcols] for ref, at in key_slots], axis=0)
            scores = lax.dot_general(
                q_two, keys, (((1,), (1,)), ((), ())), preferred_element_type=jnp.float32
            )
            scores = scores + bias_two
            top = jnp.max(scores, axis=1, keepdims=True)
            probs = jnp.exp(scores - top)
            norm = jnp.sum(probs, axis=1, keepdims=True)
            mixed = jnp.dot(
                probs.astype(jnp.bfloat16), values, preferred_element_type=jnp.float32
            ) / norm
            attended[:, cols] = jnp.where(
                lane_low, mixed[:block_len], mixed[block_len:]
            ).astype(jnp.bfloat16)

        @pl.when(j == 0)
        def _():
            w_copies[1].wait()

        att = attended[...]
        for chunk in range(0, width, 512):
            hidden[:, chunk : chunk + 512] += jnp.dot(
                att, wout[:, chunk : chunk + 512], preferred_element_type=jnp.float32
            )
        lifted = (rms_normed(hidden[...]) * gain2_ref[...]).astype(jnp.bfloat16)

        @pl.when(j == 0)
        def _():
            w_copies[2].wait()

        for chunk in range(0, hid, 512):
            activated[:, chunk : chunk + 512] = jax.nn.gelu(
                jnp.dot(lifted, wup[:, chunk : chunk + 512], preferred_element_type=jnp.float32)
            ).astype(jnp.bfloat16)

        @pl.when(j == 0)
        def _():
            w_copies[3].wait()

        act = activated[...]
        for part in range(PARTS):
            cols = slice(part * part_width, (part + 1) * part_width)
            xout[j, part] = (
                hidden[:, cols]
                + jnp.dot(act, wdown[:, cols], preferred_element_type=jnp.float32)
            ).astype(jnp.bfloat16)

            @pl.when(s < last)
            def _():
                x_copy(j, part).start()

        @pl.when(s == last)
        def _():
            final = jnp.concatenate([xout[j, part] for part in range(PARTS)], axis=1)
            final = rms_normed(final.astype(jnp.float32))
            logits = jnp.sum(final * whead_ref[...], axis=1, keepdims=True)
            spin_col = jnp.sum(
                jnp.where(col_at == row_at, spins_row(block), 0.0), axis=1, keepdims=True
            )
            signed = (1.0 - 2.0 * spin_col) * logits
            soft = jnp.maximum(signed, 0.0) + jnp.log1p(jnp.exp(-jnp.abs(signed)))
            terms = math.log(2.0) - soft
            running = jnp.sum(jnp.where(row_at <= col_at, terms, 0.0), axis=0, keepdims=True)
            total = jnp.sum(terms, axis=0, keepdims=True)
            rows_keep[j] = jnp.broadcast_to(running, (8, LANES))
            totals_send[j] = jnp.broadcast_to(total, (8, LANES))
            total_copy(j).start()

        return carry

    lax.fori_loop(0, ticks, tick, 0)

    def result_copy(j, section, ctx):
        return remote(
            result_send.at[j], result_in, res_send_sem.at[j], res_recv_sem, section, ctx
        )

    @pl.when(s == last)
    def _():
        offset = jnp.zeros((8, LANES), jnp.float32)
        for j in range(ticks):
            total_copy(j).wait_recv()
            own_total = totals_send[j]
            far_total = totals_far[j]
            before = offset + far_total * c.astype(jnp.float32)
            result = 0.5 * (rows_keep[j] + before)
            result_send[j] = result
            offset = offset + (own_total + far_total)
            to_self = (n == last) & (j == last)

            @pl.when(to_self)
            def _():
                result_in[...] = result

            @pl.when(jnp.logical_not(to_self))
            def _():
                result_copy(j, n, j * CORES + c).start()

    @pl.when(jnp.logical_not(from_self))
    def _():
        result_copy(0, s, partner).wait_recv()

    out_ref[...] = result_in[0:1, :]

    for step in range(1, groups):
        mask_copy(step).wait_send()

    @pl.when(s == 0)
    def _():
        for step in range(1, groups):
            pos_copy(step).wait_send()

    for j in range(ticks):
        @pl.when((c == 0) | (j < ticks - 1))
        def _():
            kv_copy(j).wait_send()

        @pl.when(s < last)
        def _():
            for part in range(PARTS):
                x_copy(j, part).wait_send()

        @pl.when(s == last)
        def _():
            total_copy(j).wait_send()

            @pl.when(jnp.logical_not((n == last) & (j == last)))
            def _():
                result_copy(j, n, j * CORES + c).wait_send()


def body(
    spins,
    block_mask,
    tok_embed,
    pos_embed,
    norm1_gain,
    w_qkv,
    w_out,
    norm2_gain,
    w_up,
    w_down,
    w_head,
):
    sections = lax.axis_size("section")
    ctx_count = lax.axis_size("ctx")
    ticks = ctx_count // CORES
    block_len, width = pos_embed.shape
    hid = w_up.shape[2]
    assert ticks == sections == spins.shape[0] and block_len == LANES
    bf16, f32 = jnp.bfloat16, jnp.float32
    vmem = pl.BlockSpec(memory_space=pltpu.VMEM)
    hbm = pl.BlockSpec(memory_space=pltpu.HBM)
    back = 1 << (NDIL - 2)
    dma = pltpu.SemaphoreType.DMA
    return pl.pallas_call(
        functools.partial(kernel, sections, ctx_count),
        out_shape=jax.ShapeDtypeStruct((1, block_len), f32),
        in_specs=[vmem, vmem, vmem, hbm, vmem, hbm, hbm, vmem, hbm, hbm, vmem],
        out_specs=vmem,
        scratch_shapes=[
            pltpu.VMEM((width, 3 * width), bf16),
            pltpu.VMEM((width, width), bf16),
            pltpu.VMEM((width, hid), bf16),
            pltpu.VMEM((hid, width), bf16),
            pltpu.VMEM((ticks, block_len, width), bf16),
            pltpu.VMEM((ticks, PARTS, block_len, width // PARTS), bf16),
            pltpu.VMEM((ticks, PARTS, block_len, width // PARTS), bf16),
            pltpu.VMEM((ticks + back, block_len, 2 * width), bf16),
            pltpu.VMEM((ticks + 1, block_len, 2 * width), bf16),
            pltpu.VMEM((block_len, width), bf16),
            pltpu.VMEM((block_len, width), bf16),
            pltpu.VMEM((block_len, hid), bf16),
            pltpu.VMEM((block_len, width), f32),
            pltpu.VMEM((block_len, (NDIL + 1) * block_len), f32),
            pltpu.VMEM((8, LANES), f32),
            pltpu.VMEM((ticks, 8, LANES), f32),
            pltpu.VMEM((ticks, 8, LANES), f32),
            pltpu.VMEM((ticks, 8, LANES), f32),
            pltpu.VMEM((ticks, 8, LANES), f32),
            pltpu.VMEM((ticks, 8, LANES), f32),
            pltpu.VMEM((8, LANES), f32),
            dma((4,)),
            dma,
            dma((ticks,)),
            dma((ticks,)),
            dma((ticks,)),
            dma((ticks,)),
            dma((ticks, PARTS)),
            dma((ticks, PARTS)),
            dma((ticks,)),
            dma((ticks + 1,)),
            dma((ticks,)),
            dma((ticks,)),
            dma((ticks,)),
            dma,
        ],
        compiler_params=pltpu.CompilerParams(
            collective_id=0, has_side_effects=True, vmem_limit_bytes=56 * 1024 * 1024
        ),
        cost_estimate=pl.CostEstimate(
            flops=2 * ticks * block_len * (4 * width * width + 2 * width * hid),
            bytes_accessed=2 * (4 * width * width + 2 * width * hid),
            transcendentals=0,
        ),
    )(
        spins,
        block_mask,
        tok_embed,
        pos_embed,
        norm1_gain,
        w_qkv,
        w_out,
        norm2_gain,
        w_up,
        w_down,
        w_head[None, :],
    )


def solution(mesh):
    return jax.shard_map(
        body,
        mesh=mesh,
        in_specs=(
            P(),
            P("ctx", None),
            P(),
            P("ctx", None),
            P("section", None),
            P("section", None, None),
            P("section", None, None),
            P("section", None),
            P("section", None, None),
            P("section", None, None),
            P(),
        ),
        out_specs=P("section", "ctx"),
        check_vma=False,
    )
```

time: 536 us -> 88.5 us (0.17)
  waiting for transfers between devices: 226 us -> 0 us
  starting transfers between devices: 140 us -> 0 us
  Pallas kernels: 0 us -> 85.7 us
  matrix products: 64 us -> 0 us
  local copies, waits for them, and re-layouts: 43.4 us -> 1.19 us
  other arithmetic: 33.3 us -> 0 us
  blocking collectives: 12.4 us -> 0 us
  loops' own time: 11.8 us -> 0 us
    ppermute x56 -> x0, waiting for transfers between devices: 226 us -> none  [from_behind(): return lax.ppermute(value, axis, pairs)]
    ppermute x56 -> x0, starting transfers between devices: 140 us -> none  [from_behind(): return lax.ppermute(value, axis, pairs)]
    pallas_call x0 -> x1, Pallas kernels: none -> 85.7 us  [body(): pl.pallas_call(functools.partial(kernel, sections, ctx_count), out_shape=...]
    dot_general x27 -> x0, matrix products: 64 us -> none  [the longest x4 23.2 us: finish(): jnp.dot(activated, weight_down, preferred_element_type=jnp.float32)]
    sub x4 -> x0, other arithmetic: 14.5 us -> none  [finish(): weights = jax.nn.softmax(scores, axis=-1).astype(jnp.bfloat16)]
    all_gather x1 -> x0, blocking collectives: 12.4 us -> none  [body(): lax.all_gather(totals, 'ctx', axis=0, tiled=True)]
    another operation x15 -> x0, loops' own time: 11.8 us -> none  [the longest x1 11.2 us: body(): lax.scan(section_step, initial, jnp.arange(tick_count, dtype=jnp.int32))]
    reduce_sum x9 -> x0, other arithmetic: 11 us -> none  [the longest x7 8.92 us: rms_normed(): jnp.mean(vector * vector, axis=-1, keepdims=True) + 1e-05]
  transfers between devices with their start and end apart: 56 -> 0, of which waited for: 26 -> 0; matrix products, arithmetic and copies ran while one was open for 14% -> 0% of each run, Pallas kernels for 0% -> 0%
where the time goes in v1:
time: 88.5 us; the launch traced here: 86.9 us
  Pallas kernels  85.7 us (97%)
  local copies, waits for them, and re-layouts  1.19 us (1%)
    pallas_call x1, Pallas kernels, body(): pl.pallas_call(functools.partial(kernel, sections, ctx_count), out_shape=...  85.7 us

profile of v1, /device:TPU:29, one launch (start us, length us, event | category | flops | bytes accessed | tf_op | source)
XLA Modules:
  0.0 86.9 jit_solution(2702915832080486831)
XLA Ops:
  0.0 85.7 %shard_map.109 = f32[1,128]{1,0:T(1,128)} custom-call(s32[4,1024]{1,0:T(4,128)} %spins_ref.1, s32[1,8]{1,0:T(1,128)} %mask_ref.1, f32[3,1024]{1,0:T(4,128)} %tok_ref.1, bf16[128,1024]{1,0:T(8,128)(2,1)} %pos_hbm.1, f32[1,1024]{1,0:T(1,128)} %gain1_ref.1, bf16[1,1024,3072]{2,1,0:T(8,128)(2,1)} %wqkv_hbm.1, bf16[1,1024,1024]{2,1,0:T(8,128)(2,1)} %wout_hbm.1, ...), custom_call_target="tpu_custom_call" | custom-call | flops 8589934592 | bytes 16777216 | tf_op jit(solution)/shard_map/pallas_call | solution.py:460
  85.7 1.2 %copy.13 = f32[1,128]{1,0:T(1,128)} copy(f32[1,128]{1,0:T(1,128)} %shard_map.109) | data formatting | bytes 1024

commit v2 on v1

--- a/solution.py
+++ b/solution.py
@@ -12,6 +12,7 @@
 NDIL = 3
 CORES = 2
 LANES = 128
+SOURCES = 2
 PARTS = 2
 MASKED = -1e30
 
@@ -113,6 +114,12 @@
     for step in range(1, groups):
         greet(s, ring(step) * CORES + c)
 
+    @pl.when(s == 0)
+    def _():
+        for source in range(1, SOURCES):
+            for step in range(1, groups):
+                greet(source, ring(step) * CORES + c)
+
     @pl.when(s > 0)
     def _():
         greet(s - 1, b)
@@ -129,14 +136,14 @@
     mask_send[0:1, 0:ctx_count] = mask_ref[...].astype(jnp.float32)
     mask_rows[n] = mask_send[...]
 
-    blank = jnp.zeros((block_len, 2 * width), jnp.bfloat16)
+    blank = jnp.zeros((2, block_len, width), jnp.bfloat16)
     for slot in range(1 << (NDIL - 2)):
         kv_own[slot] = blank
     kv_far[0] = blank
 
     receivers = groups + jnp.where(
         s < last, 1, ticks - jnp.where(n == last, 1, 0)
-    )
+    ) + jnp.where((s > 0) & (s < SOURCES), groups - 1, 0)
     pl.semaphore_wait(barrier, receivers)
 
     def remote(src, dst, send_sem, recv_sem, section, ctx):
@@ -155,27 +162,37 @@
             s, ring(step) * CORES + c,
         )
 
-    def pos_copy(step):
-        return remote(
-            pos_hbm, pos.at[n], pos_send_sem.at[step], pos_recv_sem.at[n],
+    share = block_len // SOURCES
+
+    def pos_copy(step, source):
+        rows = pl.ds(source * share, share)
+        return remote(
+            pos_hbm.at[rows], pos.at[n, rows], pos_send_sem.at[step], pos_recv_sem.at[n, source],
             0, ring(step) * CORES + c,
         )
 
     for step in range(1, groups):
         mask_copy(step).start()
 
-    @pl.when(s == 0)
-    def _():
-        for step in range(1, groups):
-            pos_copy(step).start()
+    for source in range(SOURCES):
+        now = (s == source) & (n == 0) if source == 0 else s == source
+
+        @pl.when(now)
+        def _():
+            for step in range(1, groups):
+                pos_copy(step, source).start()
 
     def mask_arrival(slot):
         return remote(
             mask_send, mask_rows.at[slot], mask_send_sem.at[0], mask_recv_sem.at[slot], s, partner
         )
 
-    def pos_arrival(slot):
-        return remote(pos_hbm, pos.at[slot], pos_send_sem.at[0], pos_recv_sem.at[slot], 0, partner)
+    def pos_arrival(slot, source):
+        rows = pl.ds(source * share, share)
+        return remote(
+            pos_hbm.at[rows], pos.at[slot, rows], pos_send_sem.at[0], pos_recv_sem.at[slot, source],
+            0, partner,
+        )
 
     def x_copy(j, part):
         return remote(
@@ -183,15 +200,16 @@
             s + 1, b,
         )
 
-    def kv_copy(j):
-        return remote(
-            kv_own.at[j + (1 << (NDIL - 2))], kv_far.at[j + 1], kv_send_sem.at[j],
-            kv_recv_sem.at[j + 1], s, partner,
-        )
-
-    def kv_arrival(slot):
-        return remote(
-            kv_far.at[slot], kv_far.at[slot], kv_send_sem.at[0], kv_recv_sem.at[slot], s, partner
+    def kv_copy(j, half):
+        return remote(
+            kv_own.at[j + (1 << (NDIL - 2)), half], kv_far.at[j + 1, half],
+            kv_send_sem.at[j, half], kv_recv_sem.at[j + 1, half], s, partner,
+        )
+
+    def kv_arrival(slot, half):
+        return remote(
+            kv_far.at[slot, half], kv_far.at[slot, half], kv_send_sem.at[0, half],
+            kv_recv_sem.at[slot, half], s, partner,
         )
 
     def total_copy(j):
@@ -216,14 +234,14 @@
             mask_arrival(j).wait_recv()
 
         flags = mask_rows[j]
-        bias[:, 0:block_len] = jnp.where(col_at <= row_at, 0.0, MASKED)
+        bias[0:block_len] = jnp.where(row_at <= col_at, 0.0, MASKED).astype(jnp.bfloat16)
         for level in range(NDIL):
             source = block - (1 << level)
             hit = jnp.where((lane == source) & (flags > 0.5), 1.0, 0.0)
             hit = jnp.sum(hit[0:1], axis=1, keepdims=True)
-            bias[:, (level + 1) * block_len : (level + 2) * block_len] = jnp.broadcast_to(
+            bias[(level + 1) * block_len : (level + 2) * block_len] = jnp.broadcast_to(
                 jnp.where(hit > 0.5, 0.0, MASKED), (block_len, block_len)
-            )
+            ).astype(jnp.bfloat16)
 
         @pl.when(s == 0)
         def _():
@@ -233,7 +251,13 @@
 
             @pl.when(j != n)
             def _():
-                pos_arrival(j).wait_recv()
+                for source in range(SOURCES):
+                    pos_arrival(j, source).wait_recv()
+
+            @pl.when((j == 0) & (n > 0))
+            def _():
+                for step in range(1, groups):
+                    pos_copy(step, 0).start()
 
             row = spins_row(block)
             before = spins_row(jnp.maximum(block - 1, 0))[:, block_len - 1 : block_len]
@@ -267,55 +291,84 @@
             w_copies[0].wait()
 
         own = j + (1 << (NDIL - 2))
-        for chunk in range(width, 3 * width, 512):
-            kv_own[own, :, chunk - width : chunk - width + 512] = jnp.dot(
-                normed, wqkv[:, chunk : chunk + 512], preferred_element_type=jnp.float32
-            ).astype(jnp.bfloat16)
-
-        @pl.when((c == 0) | (j < ticks - 1))
-        def _():
-            kv_copy(j).start()
+        for half in range(2):
+            for chunk in range(0, width, 512):
+                at = (half + 1) * width + chunk
+                kv_own[own, half, :, chunk : chunk + 512] = jnp.dot(
+                    normed, wqkv[:, at : at + 512], preferred_element_type=jnp.float32
+                ).astype(jnp.bfloat16)
+
+            @pl.when((c == 0) | (j < ticks - 1))
+            def _():
+                kv_copy(j, half).start()
 
         for chunk in range(0, width, 512):
             queries[:, chunk : chunk + 512] = (
                 jnp.dot(normed, wqkv[:, chunk : chunk + 512], preferred_element_type=jnp.float32)
-                .astype(jnp.bfloat16)
-                .astype(jnp.float32)
-                * (1.0 / math.sqrt(head_dim))
+                * (math.log2(math.e) / math.sqrt(head_dim))
             ).astype(jnp.bfloat16)
 
         @pl.when(j + c > 0)
         def _():
-            kv_arrival(j + c).wait_recv()
+            for half in range(2):
+                kv_arrival(j + c, half).wait_recv()
+
+        lane_low = lax.broadcasted_iota(jnp.int32, (block_len, LANES), 1) < head_dim
+        one_hot = jnp.where(row_at == col_at, 1.0, 0.0).astype(jnp.bfloat16)
+        one_hot = jnp.concatenate([one_hot, one_hot], axis=0)
+
+        def attend(slots):
+            pairs = width // LANES
+            biases = bias[0 : len(slots) * block_len]
+            ones = jnp.ones((len(slots) * block_len, LANES), jnp.bfloat16)
+
+            def scores_of(pair):
+                cols = slice(pair * LANES, (pair + 1) * LANES)
+                q_pair = queries[:, cols]
+                zero = jnp.zeros_like(q_pair)
+                q_two = jnp.concatenate(
+                    [jnp.where(lane_low, q_pair, zero), jnp.where(lane_low, zero, q_pair)], axis=0
+                )
+                keys = jnp.concatenate([ref[at, 0, :, cols] for ref, at in slots], axis=0)
+                return lax.dot_general(
+                    jnp.concatenate([q_two, one_hot], axis=1),
+                    jnp.concatenate([keys, biases], axis=1),
+                    (((1,), (1,)), ((), ())),
+                    preferred_element_type=jnp.float32,
+                )
+
+            pending = scores_of(0)
+            for pair in range(pairs):
+                cols = slice(pair * LANES, (pair + 1) * LANES)
+                scores = pending
+                if pair + 1 < pairs:
+                    pending = scores_of(pair + 1)
+                top = jnp.max(scores, axis=1, keepdims=True)
+                probs = jnp.exp2(scores - top).astype(jnp.bfloat16)
+                values = jnp.concatenate([ref[at, 1, :, cols] for ref, at in slots], axis=0)
+                mixed = jnp.dot(
+                    probs,
+                    jnp.concatenate([values, ones], axis=1),
+                    preferred_element_type=jnp.float32,
+                )
+                mixed = jnp.where(
+                    jnp.concatenate([lane_low, lane_low], axis=1),
+                    mixed[:block_len],
+                    mixed[block_len:],
+                )
+                attended[:, cols] = (mixed[:, :LANES] / mixed[:, LANES:]).astype(jnp.bfloat16)
 
         key_slots = [(kv_own, own), (kv_far, j + c)]
         for level in range(1, NDIL):
             key_slots.append((kv_own, own - (1 << (level - 1))))
-        bias_two = jnp.concatenate([bias[...], bias[...]], axis=0)
-        lane_low = lax.broadcasted_iota(jnp.int32, (block_len, LANES), 1) < head_dim
-        for pair in range(width // LANES):
-            cols = slice(pair * LANES, (pair + 1) * LANES)
-            vcols = slice(width + pair * LANES, width + (pair + 1) * LANES)
-            q_pair = queries[:, cols]
-            zero = jnp.zeros_like(q_pair)
-            q_two = jnp.concatenate(
-                [jnp.where(lane_low, q_pair, zero), jnp.where(lane_low, zero, q_pair)], axis=0
-            )
-            keys = jnp.concatenate([ref[at, :, cols] for ref, at in key_slots], axis=0)
-            values = jnp.concatenate([ref[at, :, vcols] for ref, at in key_slots], axis=0)
-            scores = lax.dot_general(
-                q_two, keys, (((1,), (1,)), ((), ())), preferred_element_type=jnp.float32
-            )
-            scores = scores + bias_two
-            top = jnp.max(scores, axis=1, keepdims=True)
-            probs = jnp.exp(scores - top)
-            norm = jnp.sum(probs, axis=1, keepdims=True)
-            mixed = jnp.dot(
-                probs.astype(jnp.bfloat16), values, preferred_element_type=jnp.float32
-            ) / norm
-            attended[:, cols] = jnp.where(
-                lane_low, mixed[:block_len], mixed[block_len:]
-            ).astype(jnp.bfloat16)
+
+        @pl.when(j == 0)
+        def _():
+            attend(key_slots[:2])
+
+        @pl.when(j > 0)
+        def _():
+            attend(key_slots)
 
         @pl.when(j == 0)
         def _():
@@ -409,15 +462,17 @@
     for step in range(1, groups):
         mask_copy(step).wait_send()
 
-    @pl.when(s == 0)
-    def _():
-        for step in range(1, groups):
-            pos_copy(step).wait_send()
+    for source in range(SOURCES):
+        @pl.when(s == source)
+        def _():
+            for step in range(1, groups):
+                pos_copy(step, source).wait_send()
 
     for j in range(ticks):
         @pl.when((c == 0) | (j < ticks - 1))
         def _():
-            kv_copy(j).wait_send()
+            for half in range(2):
+                kv_copy(j, half).wait_send()
 
         @pl.when(s < last)
         def _():
@@ -470,13 +525,13 @@
             pltpu.VMEM((ticks, block_len, width), bf16),
             pltpu.VMEM((ticks, PARTS, block_len, width // PARTS), bf16),
             pltpu.VMEM((ticks, PARTS, block_len, width // PARTS), bf16),
-            pltpu.VMEM((ticks + back, block_len, 2 * width), bf16),
-            pltpu.VMEM((ticks + 1, block_len, 2 * width), bf16),
+            pltpu.VMEM((ticks + back, 2, block_len, width), bf16),
+            pltpu.VMEM((ticks + 1, 2, block_len, width), bf16),
             pltpu.VMEM((block_len, width), bf16),
             pltpu.VMEM((block_len, width), bf16),
             pltpu.VMEM((block_len, hid), bf16),
             pltpu.VMEM((block_len, width), f32),
-            pltpu.VMEM((block_len, (NDIL + 1) * block_len), f32),
+            pltpu.VMEM(((NDIL + 1) * block_len, block_len), bf16),
             pltpu.VMEM((8, LANES), f32),
             pltpu.VMEM((ticks, 8, LANES), f32),
             pltpu.VMEM((ticks, 8, LANES), f32),
@@ -487,13 +542,13 @@
             dma((4,)),
             dma,
             dma((ticks,)),
-            dma((ticks,)),
+            dma((ticks, SOURCES)),
             dma((ticks,)),
             dma((ticks,)),
             dma((ticks, PARTS)),
             dma((ticks, PARTS)),
-            dma((ticks,)),
-            dma((ticks + 1,)),
+            dma((ticks, 2)),
+            dma((ticks + 1, 2)),
             dma((ticks,)),
             dma((ticks,)),
             dma((ticks,)),

time: 88.5 us -> 83.3 us (0.941)
  Pallas kernels: 85.7 us -> 80.5 us
    pallas_call x1, Pallas kernels: 85.7 us -> 80.5 us  [body(): pl.pallas_call(functools.partial(kernel, sections, ctx_count), out_shape=...]
where the time goes in v2:
time: 83.3 us; the launch traced here: 81.7 us
  Pallas kernels  80.5 us (97%)
  local copies, waits for them, and re-layouts  1.19 us (1%)
    pallas_call x1, Pallas kernels, body(): pl.pallas_call(functools.partial(kernel, sections, ctx_count), out_shape=...  80.5 us

profile of v2, /device:TPU:29, one launch (start us, length us, event | category | flops | bytes accessed | tf_op | source)
XLA Modules:
  0.0 81.7 jit_solution(13816461037662726132)
XLA Ops:
  0.0 80.5 %shard_map.109 = f32[1,128]{1,0:T(1,128)} custom-call(s32[4,1024]{1,0:T(4,128)} %spins_ref.1, s32[1,8]{1,0:T(1,128)} %mask_ref.1, f32[3,1024]{1,0:T(4,128)} %tok_ref.1, bf16[128,1024]{1,0:T(8,128)(2,1)} %pos_hbm.1, f32[1,1024]{1,0:T(1,128)} %gain1_ref.1, bf16[1,1024,3072]{2,1,0:T(8,128)(2,1)} %wqkv_hbm.1, bf16[1,1024,1024]{2,1,0:T(8,128)(2,1)} %wout_hbm.1, ...), custom_call_target="tpu_custom_call" | custom-call | flops 8589934592 | bytes 16777216 | tf_op jit(solution)/shard_map/pallas_call | solution.py:515
  80.5 1.2 %copy.13 = f32[1,128]{1,0:T(1,128)} copy(f32[1,128]{1,0:T(1,128)} %shard_map.109) | data formatting | bytes 1024

commit v3 on v2

--- a/solution.py
+++ b/solution.py
@@ -10,6 +10,7 @@
 
 HEADS = 16
 NDIL = 3
+COLS = 1024
 CORES = 2
 LANES = 128
 SOURCES = 2
@@ -71,6 +72,8 @@
     tot_recv_sem,
     res_send_sem,
     res_recv_sem,
+    turn_sem,
+    offset,
 ):
     ticks = ctx_count // CORES
     groups = ticks
@@ -175,12 +178,24 @@
         mask_copy(step).start()
 
     for source in range(SOURCES):
+        @pl.when((s == source) & (n == 0) & (c == 1))
+        def _():
+            pl.semaphore_wait(turn_sem, 1)
+
         now = (s == source) & (n == 0) if source == 0 else s == source
 
         @pl.when(now)
         def _():
             for step in range(1, groups):
                 pos_copy(step, source).start()
+
+        @pl.when((s == source) & (n == 0) & (c == 0))
+        def _():
+            for step in range(1, groups):
+                pos_copy(step, source).wait_send()
+            pl.semaphore_signal(
+                turn_sem, inc=1, device_id=(s, partner), device_id_type=pl.DeviceIdType.MESH
+            )
 
     def mask_arrival(slot):
         return remote(
@@ -228,20 +243,6 @@
 
     def tick(j, carry):
         block = j * CORES + c
-
-        @pl.when(j != n)
-        def _():
-            mask_arrival(j).wait_recv()
-
-        flags = mask_rows[j]
-        bias[0:block_len] = jnp.where(row_at <= col_at, 0.0, MASKED).astype(jnp.bfloat16)
-        for level in range(NDIL):
-            source = block - (1 << level)
-            hit = jnp.where((lane == source) & (flags > 0.5), 1.0, 0.0)
-            hit = jnp.sum(hit[0:1], axis=1, keepdims=True)
-            bias[(level + 1) * block_len : (level + 2) * block_len] = jnp.broadcast_to(
-                jnp.where(hit > 0.5, 0.0, MASKED), (block_len, block_len)
-            ).astype(jnp.bfloat16)
 
         @pl.when(s == 0)
         def _():
@@ -286,25 +287,29 @@
         hidden[...] = layer_in
         normed = (rms_normed(layer_in) * gain1_ref[...]).astype(jnp.bfloat16)
 
-        @pl.when(j == 0)
-        def _():
-            w_copies[0].wait()
+        flags = mask_rows[j]
+        bias[0:block_len] = jnp.where(row_at <= col_at, 0.0, MASKED).astype(jnp.bfloat16)
+        for level in range(NDIL):
+            source = block - (1 << level)
+            hit = jnp.where((lane == source) & (flags > 0.5), 1.0, 0.0)
+            hit = jnp.sum(hit[0:1], axis=1, keepdims=True)
+            bias[(level + 1) * block_len : (level + 2) * block_len] = jnp.broadcast_to(
+                jnp.where(hit > 0.5, 0.0, MASKED), (block_len, block_len)
+            ).astype(jnp.bfloat16)
 
         own = j + (1 << (NDIL - 2))
         for half in range(2):
-            for chunk in range(0, width, 512):
+            for chunk in range(0, width, COLS):
                 at = (half + 1) * width + chunk
-                kv_own[own, half, :, chunk : chunk + 512] = jnp.dot(
-                    normed, wqkv[:, at : at + 512], preferred_element_type=jnp.float32
+                kv_own[own, half, :, chunk : chunk + COLS] = jnp.dot(
+                    normed, wqkv[:, at : at + COLS], preferred_element_type=jnp.float32
                 ).astype(jnp.bfloat16)
 
-            @pl.when((c == 0) | (j < ticks - 1))
-            def _():
-                kv_copy(j, half).start()
-
-        for chunk in range(0, width, 512):
-            queries[:, chunk : chunk + 512] = (
-                jnp.dot(normed, wqkv[:, chunk : chunk + 512], preferred_element_type=jnp.float32)
+            kv_copy(j, half).start()
+
+        for chunk in range(0, width, COLS):
+            queries[:, chunk : chunk + COLS] = (
+                jnp.dot(normed, wqkv[:, chunk : chunk + COLS], preferred_element_type=jnp.float32)
                 * (math.log2(math.e) / math.sqrt(head_dim))
             ).astype(jnp.bfloat16)
 
@@ -370,29 +375,17 @@
         def _():
             attend(key_slots)
 
-        @pl.when(j == 0)
-        def _():
-            w_copies[1].wait()
-
         att = attended[...]
-        for chunk in range(0, width, 512):
-            hidden[:, chunk : chunk + 512] += jnp.dot(
-                att, wout[:, chunk : chunk + 512], preferred_element_type=jnp.float32
+        for chunk in range(0, width, COLS):
+            hidden[:, chunk : chunk + COLS] += jnp.dot(
+                att, wout[:, chunk : chunk + COLS], preferred_element_type=jnp.float32
             )
         lifted = (rms_normed(hidden[...]) * gain2_ref[...]).astype(jnp.bfloat16)
 
-        @pl.when(j == 0)
-        def _():
-            w_copies[2].wait()
-
-        for chunk in range(0, hid, 512):
-            activated[:, chunk : chunk + 512] = jax.nn.gelu(
-                jnp.dot(lifted, wup[:, chunk : chunk + 512], preferred_element_type=jnp.float32)
+        for chunk in range(0, hid, COLS):
+            activated[:, chunk : chunk + COLS] = jax.nn.gelu(
+                jnp.dot(lifted, wup[:, chunk : chunk + COLS], preferred_element_type=jnp.float32)
             ).astype(jnp.bfloat16)
-
-        @pl.when(j == 0)
-        def _():
-            w_copies[3].wait()
 
         act = activated[...]
         for part in range(PARTS):
@@ -425,6 +418,11 @@
 
         return carry
 
+    for step in range(1, groups):
+        mask_arrival(ring(step)).wait_recv()
+    for copy in w_copies:
+        copy.wait()
+
     lax.fori_loop(0, ticks, tick, 0)
 
     def result_copy(j, section, ctx):
@@ -434,24 +432,32 @@
 
     @pl.when(s == last)
     def _():
-        offset = jnp.zeros((8, LANES), jnp.float32)
+        offset[...] = jnp.zeros((8, LANES), jnp.float32)
         for j in range(ticks):
-            total_copy(j).wait_recv()
-            own_total = totals_send[j]
-            far_total = totals_far[j]
-            before = offset + far_total * c.astype(jnp.float32)
-            result = 0.5 * (rows_keep[j] + before)
-            result_send[j] = result
-            offset = offset + (own_total + far_total)
+            @pl.when(c == 0)
+            def _():
+                result_send[j] = 0.5 * (rows_keep[j] + offset[...])
+
+            @pl.when(c == 1)
+            def _():
+                total_copy(j).wait_recv()
+                result_send[j] = 0.5 * (rows_keep[j] + (offset[...] + totals_far[j]))
+
             to_self = (n == last) & (j == last)
 
             @pl.when(to_self)
             def _():
-                result_in[...] = result
+                result_in[...] = result_send[j]
 
             @pl.when(jnp.logical_not(to_self))
             def _():
                 result_copy(j, n, j * CORES + c).start()
+
+            @pl.when(c == 0)
+            def _():
+                total_copy(j).wait_recv()
+
+            offset[...] += totals_send[j] + totals_far[j]
 
     @pl.when(jnp.logical_not(from_self))
     def _():
@@ -459,20 +465,23 @@
 
     out_ref[...] = result_in[0:1, :]
 
+    @pl.when(c == 0)
+    def _():
+        for half in range(2):
+            kv_arrival(ticks, half).wait_recv()
+
     for step in range(1, groups):
         mask_copy(step).wait_send()
 
     for source in range(SOURCES):
-        @pl.when(s == source)
+        @pl.when((s == source) & (b > 0))
         def _():
             for step in range(1, groups):
                 pos_copy(step, source).wait_send()
 
     for j in range(ticks):
-        @pl.when((c == 0) | (j < ticks - 1))
-        def _():
-            for half in range(2):
-                kv_copy(j, half).wait_send()
+        for half in range(2):
+            kv_copy(j, half).wait_send()
 
         @pl.when(s < last)
         def _():
@@ -553,6 +562,8 @@
             dma((ticks,)),
             dma((ticks,)),
             dma,
+            pltpu.SemaphoreType.REGULAR,
+            pltpu.VMEM((8, LANES), f32),
         ],
         compiler_params=pltpu.CompilerParams(
             collective_id=0, has_side_effects=True, vmem_limit_bytes=56 * 1024 * 1024

time: 83.3 us -> 75.9 us (0.911)
  the two profiles are of different devices: /device:TPU:29 before, /device:TPU:0 now
where the time goes in v3:
time: 75.9 us; the launch traced here: 75.7 us
  Pallas kernels  74.5 us (98%)
  local copies, waits for them, and re-layouts  1.19 us (2%)
    pallas_call x1, Pallas kernels, body(): pl.pallas_call(functools.partial(kernel, sections, ctx_count), out_shape=...  74.5 us

profile of v3, /device:TPU:0, one launch (start us, length us, event | category | flops | bytes accessed | tf_op | source)
XLA Modules:
  0.0 75.7 jit_solution(6408128464797791051)
XLA Ops:
  0.0 74.5 %shard_map.109 = f32[1,128]{1,0:T(1,128)} custom-call(s32[4,1024]{1,0:T(4,128)} %spins_ref.1, s32[1,8]{1,0:T(1,128)} %mask_ref.1, f32[3,1024]{1,0:T(4,128)} %tok_ref.1, bf16[128,1024]{1,0:T(8,128)(2,1)} %pos_hbm.1, f32[1,1024]{1,0:T(1,128)} %gain1_ref.1, bf16[1,1024,3072]{2,1,0:T(8,128)(2,1)} %wqkv_hbm.1, bf16[1,1024,1024]{2,1,0:T(8,128)(2,1)} %wout_hbm.1, ...), custom_call_target="tpu_custom_call" | custom-call | flops 8589934592 | bytes 16777216 | tf_op jit(solution)/shard_map/pallas_call | solution.py:524
  74.5 1.2 %copy.13 = f32[1,128]{1,0:T(1,128)} copy(f32[1,128]{1,0:T(1,128)} %shard_map.109) | data formatting | bytes 1024
